TPU v7x, 32 devices: a whole 2x2x4 slice. The times are simulated.
32 devices in a mesh: rep: 4 (over y, x), seq: 4 (over z), shard: 2 (over core).
Axes of the slice: x: 2, y: 2, z: 4, core: 2. Of those that a mesh axis runs over, the one named last changes fastest.
Arguments:
- tokens: bfloat16 [8, 1024, 768], P(('rep', 'shard'), 'seq'), may hold values from -6 to 6
- out_grad: bfloat16 [8, 1024, 768], P(('rep', 'shard'), 'seq'), may hold values from -6 to 6
- attention_gain: bfloat16 [768], P(('seq', 'shard')), may hold values from 0.099609375 to 1.8984375
- query_weight: bfloat16 [768, 768], P(('seq', 'shard')), may hold values from -0.02734375 to 0.02734375
- key_weight: bfloat16 [768, 768], P(('seq', 'shard')), may hold values from -0.21875 to 0.21875
- value_weight: bfloat16 [768, 768], P(('seq', 'shard')), may hold values from -0.21875 to 0.21875
- output_weight: bfloat16 [768, 768], P(('seq', 'shard')), may hold values from -3.5 to 3.5
- position_bias: bfloat16 [384], P(('seq', 'shard')), may hold values from -4 to 4
- bucket_table: int32 [2047], replicated, may hold values from 0 to 31
- feedforward_gain: bfloat16 [768], P(('seq', 'shard')), may hold values from 0.099609375 to 1.8984375
- router_matrix: bfloat16 [768, 8], P(('seq', 'shard')), may hold values from -0.109375 to 0.109375
- routes: int32 [8, 1024, 1], P(('rep', 'shard'), 'seq'), may hold values from 0 to 7; in each aligned block of 256 rows (0 to 255, 256 to 511, ..., all dimensions but the last counted through in order) at most 64 rows name the same one
- up_weight: bfloat16 [8, 3072, 768], P(('seq', 'shard'), 'rep'), may hold values from -0.21875 to 0.21875
- down_weight: bfloat16 [8, 3072, 768], P(('seq', 'shard'), 'rep'), may hold values from -4 to 4
Outputs:
- layer_output: bfloat16 [8, 1024, 768], P(('rep', 'shard'), 'seq')
- token_input_gradient: float32 [8, 1024, 768], P(('rep', 'shard'), 'seq')
- attention_gain_grad: float32 [768], P(('seq', 'shard'))
- query_weight_grad: float32 [768, 768], P(('seq', 'shard'))
- key_weight_grad: float32 [768, 768], P(('seq', 'shard'))
- value_weight_grad: float32 [768, 768], P(('seq', 'shard'))
- output_weight_grad: float32 [768, 768], P(('seq', 'shard'))
- position_bias_grad: float32 [384], P(('seq', 'shard'))
- feedforward_gain_grad: float32 [768], P(('seq', 'shard'))
- router_weight_grad: float32 [768, 8], P(('seq', 'shard'))
- up_weight_grad: float32 [8, 3072, 768], P(('seq', 'shard'), 'rep')
- down_weight_grad: float32 [8, 3072, 768], P(('seq', 'shard'), 'rep')
Inputs may be any that keep to these rules, and one draw needn't show every extreme that they name: `routes`: in each aligned block of 256 rows in sequence order (the rows of one device) no expert is named more than 64 times, a bound that some block reaches.
All inputs are finite; a program needn't handle non-finite values.
Results may differ from a plain program's by a relative error of at most 0.02.
Values may be sent and summed in bfloat16 or wider, within the bound.
No kernel may reach another device: no remote copies, remote signals or barrier semaphores. Data moves between devices by JAX's collectives and lax.ppermute only.
A program may use at most 128 MiB of HBM per device.

v0:
```python
from functools import partial

import jax
import jax.numpy as jnp
from jax import lax
from jax.experimental import pallas as pl
from jax.experimental.pallas import tpu as pltpu
from jax.sharding import PartitionSpec as P

BUCKETS = 32
EPSILON = 1e-06
TILE = 128
VMEM_BYTES = 48 * 1024 * 1024
BF16 = jnp.bfloat16
F32 = jnp.float32


def dot_nn(left, right):
    return jnp.dot(left, right, preferred_element_type=F32)


def dot_nt(left, right):
    return lax.dot_general(left, right, (((1,), (1,)), ((), ())), preferred_element_type=F32)


def dot_tn(left, right):
    return lax.dot_general(left, right, (((0,), (0,)), ((), ())), preferred_element_type=F32)


def skew_kernel(offset_ref, skewed_ref):
    heads, width = skewed_ref.shape[0], skewed_ref.shape[2]
    row = lax.broadcasted_iota(jnp.int32, (8, width), 0)
    for head in range(heads):
        base = jnp.broadcast_to(offset_ref[head : head + 1, :], (8, width))
        part = pltpu.roll(base, width - (TILE - 1), axis=1)
        for bit in (1, 2, 4):
            part = jnp.where((row & bit) != 0, pltpu.roll(part, bit, axis=1), part)
        for step in (8, 16, 32, 64):
            part = jnp.concatenate([part, pltpu.roll(part, step, axis=1)], axis=0)
        skewed_ref[head] = part


def skew_bias(offset_bias, heads):
    width = offset_bias.shape[1]
    return pl.pallas_call(
        skew_kernel,
        out_shape=jax.ShapeDtypeStruct((heads, TILE, width), F32),
        compiler_params=pltpu.CompilerParams(vmem_limit_bytes=VMEM_BYTES),
    )(offset_bias)


def forward_kernel(
    heads, head_size, row_count, tokens_ref, gain_ref, weight_ref, skewed_ref,
    normed_ref, qkv_ref, probs_ref, context_ref, parts,
):
    block = pl.program_id(0)
    length = tokens_ref.shape[0]
    tiles = length // TILE
    width = heads * head_size

    @pl.when(block == 0)
    def _():
        values = tokens_ref[...].astype(F32)
        scale = lax.rsqrt(jnp.mean(values * values, axis=-1, keepdims=True) + EPSILON)
        normed = (values * scale * gain_ref[...]).astype(BF16)
        normed_ref[...] = normed
        for kind in range(3):
            made = dot_nn(normed, weight_ref[kind]).astype(BF16)
            qkv_ref[kind] = made
            for head in range(heads):
                parts[kind * heads + head] = made[:, head * head_size : (head + 1) * head_size]

    first = pl.multiple_of(block * row_count, row_count)
    contexts = []
    for head in range(heads):
        query = parts[head, pl.ds(first, row_count), :]
        scores = dot_nt(query, parts[heads + head])
        biases = []
        for piece in range(row_count // TILE):
            at = (tiles - 1 - piece - block * (row_count // TILE)) * TILE
            biases.append(skewed_ref[head, :, pl.ds(pl.multiple_of(at, TILE), length)])
        scores = scores + jnp.concatenate(biases, axis=0)
        peak = jnp.max(scores, axis=-1, keepdims=True)
        raised = jnp.exp(scores - peak)
        total = jnp.sum(raised, axis=-1, keepdims=True)
        probs = (raised * (1.0 / total)).astype(BF16)
        probs_ref[head] = probs
        contexts.append(dot_nn(probs, parts[2 * heads + head]))
    context_ref[...] = jnp.concatenate(contexts, axis=1).astype(BF16)


def attention_forward(tokens, gain, weight, skewed, heads, head_size):
    length, model_width = tokens.shape
    rows = 256
    width = heads * head_size
    return pl.pallas_call(
        partial(forward_kernel, heads, head_size, rows),
        grid=(length // rows,),
        in_specs=[
            pl.BlockSpec((length, model_width), lambda i: (0, 0)),
            pl.BlockSpec((1, model_width), lambda i: (0, 0)),
            pl.BlockSpec((3, model_width, width), lambda i: (0, 0, 0)),
            pl.BlockSpec(skewed.shape, lambda i: (0, 0, 0)),
        ],
        out_specs=[
            pl.BlockSpec((length, model_width), lambda i: (0, 0)),
            pl.BlockSpec((3, length, width), lambda i: (0, 0, 0)),
            pl.BlockSpec((heads, rows, length), lambda i: (0, i, 0)),
            pl.BlockSpec((rows, width), lambda i: (i, 0)),
        ],
        out_shape=[
            jax.ShapeDtypeStruct((length, model_width), BF16),
            jax.ShapeDtypeStruct((3, length, width), BF16),
            jax.ShapeDtypeStruct((heads, length, length), BF16),
            jax.ShapeDtypeStruct((length, width), BF16),
        ],
        scratch_shapes=[pltpu.VMEM((3 * heads, length, head_size), BF16)],
        compiler_params=pltpu.CompilerParams(vmem_limit_bytes=VMEM_BYTES),
        cost_estimate=pl.CostEstimate(
            flops=2 * length * model_width * 3 * width + 4 * length * length * width,
            bytes_accessed=16 * 1024 * 1024,
            transcendentals=heads * length * length,
        ),
    )(tokens, gain, weight, skewed)


def backward_kernel(
    heads, head_size, row_count, qkv_ref, probs_ref, grad_ref, weight_ref, tokens_ref, normed_ref,
    weight_grad_ref, token_grad_ref, gain_grad_ref, offset_ref,
    parts, dqueries, dkeys, dvalues, diagonals,
):
    block = pl.program_id(0)
    length = qkv_ref.shape[1]
    tiles = length // TILE
    span = diagonals.shape[2]

    @pl.when(block == 0)
    def _():
        for kind in range(3):
            made = qkv_ref[kind]
            for head in range(heads):
                parts[kind * heads + head] = made[:, head * head_size : (head + 1) * head_size]
        dkeys[...] = jnp.zeros_like(dkeys)
        dvalues[...] = jnp.zeros_like(dvalues)
        diagonals[...] = jnp.zeros_like(diagonals)

    first = pl.multiple_of(block * row_count, row_count)
    grads = grad_ref[...]
    made_queries = []
    for head in range(heads):
        query = parts[head, pl.ds(first, row_count), :]
        grad = grads[:, head * head_size : (head + 1) * head_size]
        probs_low = probs_ref[head]
        probs = probs_low.astype(F32)
        dprobs = dot_nt(grad, parts[2 * heads + head])
        delta = jnp.sum(dprobs * probs, axis=-1, keepdims=True)
        dscores = probs * (dprobs - delta)
        for piece in range(row_count // TILE):
            at = (tiles - 1 - piece - block * (row_count // TILE)) * TILE
            window = pl.ds(pl.multiple_of(at, TILE), length)
            diagonals[head, :, window] += dscores[piece * TILE : (piece + 1) * TILE]
        dscores_low = dscores.astype(BF16)
        made_queries.append(dot_nn(dscores_low, parts[heads + head]))
        dkeys[head] += dot_tn(query, dscores_low)
        dvalues[head] += dot_tn(grad, probs_low)
    dqueries[pl.ds(first, row_count), :] = jnp.concatenate(made_queries, axis=1).astype(BF16)

    @pl.when(block == pl.num_programs(0) - 1)
    def _():
        key_side = jnp.concatenate([dkeys[head] for head in range(heads)], axis=0)
        value_side = jnp.concatenate([dvalues[head] for head in range(heads)], axis=0)
        sides = (dqueries[...], key_side.T.astype(BF16), value_side.T.astype(BF16))
        normed = normed_ref[...]
        token_grad = jnp.zeros(tokens_ref.shape, F32)
        for kind in range(3):
            weight_grad_ref[kind] = dot_tn(normed, sides[kind])
            token_grad = token_grad + dot_nt(sides[kind], weight_ref[kind])
        token_grad_ref[...] = token_grad.astype(BF16)
        values = tokens_ref[...].astype(F32)
        scale = lax.rsqrt(jnp.mean(values * values, axis=-1, keepdims=True) + EPSILON)
        gain_grad_ref[...] = jnp.sum(token_grad * values * scale, axis=0, keepdims=True)
        row = lax.broadcasted_iota(jnp.int32, (8, span), 0)
        offset_ref[...] = jnp.zeros_like(offset_ref)
        for head in range(heads):
            part = diagonals[head]
            for step in (64, 32, 16, 8):
                part = part[:step] + pltpu.roll(part[step:], span - step, axis=1)
            for bit in (1, 2, 4):
                part = jnp.where((row & bit) != 0, pltpu.roll(part, span - bit, axis=1), part)
            part = pltpu.roll(part, TILE - 1, axis=1)
            offset_ref[head : head + 1, :] = jnp.sum(part, axis=0, keepdims=True)


def attention_backward(qkv, probs, grad, weight, tokens, normed, heads, head_size):
    length, model_width = tokens.shape
    rows = 256
    width = heads * head_size
    padded_heads = -(-heads // 8) * 8
    return pl.pallas_call(
        partial(backward_kernel, heads, head_size, rows),
        grid=(length // rows,),
        in_specs=[
            pl.BlockSpec((3, length, width), lambda i: (0, 0, 0)),
            pl.BlockSpec((heads, rows, length), lambda i: (0, i, 0)),
            pl.BlockSpec((rows, width), lambda i: (i, 0)),
            pl.BlockSpec((3, model_width, width), lambda i: (0, 0, 0)),
            pl.BlockSpec((length, model_width), lambda i: (0, 0)),
            pl.BlockSpec((length, model_width), lambda i: (0, 0)),
        ],
        out_specs=[
            pl.BlockSpec((3, model_width, width), lambda i: (0, 0, 0)),
            pl.BlockSpec((length, model_width), lambda i: (0, 0)),
            pl.BlockSpec((1, model_width), lambda i: (0, 0)),
            pl.BlockSpec((padded_heads, 2 * length), lambda i: (0, 0)),
        ],
        out_shape=[
            jax.ShapeDtypeStruct((3, model_width, width), F32),
            jax.ShapeDtypeStruct((length, model_width), BF16),
            jax.ShapeDtypeStruct((1, model_width), F32),
            jax.ShapeDtypeStruct((padded_heads, 2 * length), F32),
        ],
        scratch_shapes=[
            pltpu.VMEM((3 * heads, length, head_size), BF16),
            pltpu.VMEM((length, width), BF16),
            pltpu.VMEM((heads, head_size, length), F32),
            pltpu.VMEM((heads, head_size, length), F32),
            pltpu.VMEM((heads, TILE, 2 * length), F32),
        ],
        compiler_params=pltpu.CompilerParams(vmem_limit_bytes=VMEM_BYTES),
        cost_estimate=pl.CostEstimate(
            flops=8 * length * length * width + 12 * length * model_width * width,
            bytes_accessed=16 * 1024 * 1024,
            transcendentals=0,
        ),
    )(qkv, probs, grad, weight, tokens, normed)


def expert_kernel(
    experts, rows_ref, grads_ref, router_ref, picked_ref, up_ref, down_ref,
    up_grad_ref, down_grad_ref, rows_grad_ref, returned_ref, logit_grad_ref,
    out_total, in_total, router_probs, low_grads_ref,
):
    step = pl.program_id(0)
    picked = picked_ref[...]

    @pl.when(step == 0)
    def _():
        logits = dot_nn(rows_ref[...], router_ref[...])
        lane = lax.broadcasted_iota(jnp.int32, logits.shape, 1)
        peak = jnp.max(jnp.where(lane < experts, logits, -jnp.inf), axis=-1, keepdims=True)
        raised = jnp.where(lane < experts, jnp.exp(jnp.minimum(logits - peak, 0.0)), 0.0)
        probs = raised / jnp.sum(raised, axis=-1, keepdims=True)
        router_probs[...] = probs
        gate = jnp.sum(probs * picked, axis=-1, keepdims=True)
        low_grads_ref[...] = (gate * grads_ref[...].astype(F32)).astype(BF16)
        out_total[...] = jnp.zeros_like(out_total)
        in_total[...] = jnp.zeros_like(in_total)

    up = up_ref[...]
    down = down_ref[...]
    pre = dot_nt(rows_ref[...], up)
    hidden_grad = dot_nt(low_grads_ref[...], down)
    slope = 0.7978845608028654
    square = pre * pre
    curve = jnp.tanh(slope * pre * (1.0 + 0.044715 * square))
    half = 0.5 * (1.0 + curve)
    hidden = (pre * half).astype(BF16)
    derivative = half + (0.5 * slope) * pre * (1.0 - curve * curve) * (
        1.0 + (3.0 * 0.044715) * square
    )
    pre_grad = (hidden_grad * derivative).astype(BF16)
    up_grad_ref[...] = dot_tn(pre_grad, rows_ref[...]).astype(BF16)
    down_grad_ref[...] = dot_tn(hidden, low_grads_ref[...]).astype(BF16)
    out_total[...] += dot_nn(hidden, down)
    in_total[...] += dot_nn(pre_grad, up)

    @pl.when(step == pl.num_programs(0) - 1)
    def _():
        probs = router_probs[...]
        gate = jnp.sum(probs * picked, axis=-1, keepdims=True)
        out = out_total[...].astype(BF16).astype(F32)
        gate_grad = jnp.sum(grads_ref[...].astype(F32) * out, axis=-1, keepdims=True)
        logit_grad = (gate_grad * gate * (picked - probs)).astype(BF16)
        logit_grad_ref[...] = logit_grad
        rows_grad_ref[...] = (in_total[...] + dot_nt(logit_grad, router_ref[...])).astype(BF16)
        returned_ref[...] = (gate * out).astype(BF16)


def expert_pass(rows, grads, router, picked, up, down, experts):
    count, model_width = rows.shape
    units = up.shape[0]
    lanes = router.shape[1]
    block = 512
    whole = pl.BlockSpec((count, model_width), lambda i: (0, 0))
    return pl.pallas_call(
        partial(expert_kernel, experts),
        grid=(units // block,),
        in_specs=[
            whole,
            whole,
            pl.BlockSpec((model_width, lanes), lambda i: (0, 0)),
            pl.BlockSpec((1, lanes), lambda i: (0, 0)),
            pl.BlockSpec((block, model_width), lambda i: (i, 0)),
            pl.BlockSpec((block, model_width), lambda i: (i, 0)),
        ],
        out_specs=[
            pl.BlockSpec((block, model_width), lambda i: (i, 0)),
            pl.BlockSpec((block, model_width), lambda i: (i, 0)),
            whole,
            whole,
            pl.BlockSpec((count, lanes), lambda i: (0, 0)),
        ],
        out_shape=[
            jax.ShapeDtypeStruct((units, model_width), BF16),
            jax.ShapeDtypeStruct((units, model_width), BF16),
            jax.ShapeDtypeStruct((count, model_width), BF16),
            jax.ShapeDtypeStruct((count, model_width), BF16),
            jax.ShapeDtypeStruct((count, lanes), BF16),
        ],
        scratch_shapes=[
            pltpu.VMEM((count, model_width), F32),
            pltpu.VMEM((count, model_width), F32),
            pltpu.VMEM((count, lanes), F32),
            pltpu.VMEM((count, model_width), BF16),
        ],
        compiler_params=pltpu.CompilerParams(vmem_limit_bytes=VMEM_BYTES),
        cost_estimate=pl.CostEstimate(
            flops=12 * count * units * model_width,
            bytes_accessed=16 * 1024 * 1024,
            transcendentals=count * units,
        ),
    )(rows, grads, router, picked, up, down)


def inverse_rms(values):
    return lax.rsqrt(jnp.mean(values * values, axis=-1, keepdims=True) + EPSILON)


def norm_backward(values, inverse, gain, grad):
    scaled = grad * gain
    return inverse * scaled - values * (
        inverse * inverse * inverse * jnp.mean(scaled * values, axis=-1, keepdims=True)
    )


def gather_rows(rows, axis_name):
    count = lax.axis_size(axis_name)
    place = lax.axis_index(axis_name)
    height = rows.shape[0]
    whole = jnp.zeros((count * height,) + rows.shape[1:], rows.dtype)
    whole = lax.dynamic_update_slice_in_dim(whole, rows, place * height, 0)
    for shift in range(1, count):
        moved = lax.ppermute(rows, axis_name, [(j, (j + shift) % count) for j in range(count)])
        origin = lax.rem(place + count - shift, count)
        whole = lax.dynamic_update_slice_in_dim(whole, moved, origin * height, 0)
    return whole


def reduce_rows(parts, axis_name):
    count = lax.axis_size(axis_name)
    place = lax.axis_index(axis_name)
    total = lax.dynamic_index_in_dim(parts, place, 0, False).astype(F32)
    for shift in range(1, count):
        target = lax.rem(place + shift, count)
        moved = lax.ppermute(
            lax.dynamic_index_in_dim(parts, target, 0, False).astype(BF16),
            axis_name,
            [(j, (j + shift) % count) for j in range(count)],
        )
        total = total + moved.astype(F32)
    return total


def exchange_by_permutes(piece_for, axis_name):
    count = lax.axis_size(axis_name)
    place = lax.axis_index(axis_name)
    held = [piece_for(place)]
    for shift in range(1, count):
        held.append(
            lax.ppermute(
                piece_for(lax.rem(place + shift, count)),
                axis_name,
                [(j, (j + shift) % count) for j in range(count)],
            )
        )
    return [
        lax.select_n(lax.rem(place + count - origin, count), *held) for origin in range(count)
    ]


def quarters(parts, count):
    lead, rows, lanes = parts.shape
    return parts.reshape(lead, count, rows // count, lanes).transpose(1, 0, 2, 3)


def after(value, *earlier):
    return lax.optimization_barrier((value,) + earlier)[0]


def exchange(parts, axis_name):
    return lax.all_to_all(parts, axis_name, split_axis=0, concat_axis=0, tiled=True)


def per_device(
    tokens,
    out_grad,
    attention_gain,
    query_weight,
    key_weight,
    value_weight,
    output_weight,
    position_bias,
    bucket_table,
    feedforward_gain,
    router_matrix,
    routes,
    up_weight,
    down_weight,
):
    group = ("seq", "shard")
    seq_count = lax.axis_size("seq")
    shard_count = lax.axis_size("shard")
    rep_count = lax.axis_size("rep")
    seq_place = lax.axis_index("seq")
    owner_count = seq_count * shard_count
    seg_rows = tokens.shape[1]
    model_width = tokens.shape[2]
    length = seg_rows * seq_count
    head_count = position_bias.shape[0] * owner_count // BUCKETS
    head_size = model_width // head_count
    heads = head_count // seq_count
    width = heads * head_size
    experts = router_matrix.shape[1]
    capacity = 2 * seg_rows // experts
    shard_rows = query_weight.shape[0]

    token_rows = tokens[0]
    grad_rows = out_grad[0]

    small = jnp.concatenate(
        [attention_gain, feedforward_gain, position_bias, router_matrix.reshape(-1)]
    )
    small_size = small.shape[0]
    small_rows = -(-small_size // (16 * width)) * 16
    small = jnp.pad(small, (0, small_rows * width - small_size)).reshape(small_rows, width)
    stacked = jnp.concatenate([query_weight, key_weight, value_weight], axis=0)

    def weight_piece(target):
        columns = lax.dynamic_slice_in_dim(stacked, target * width, width, 1)
        return jnp.concatenate([columns, small], axis=0)

    packed = jnp.stack(exchange_by_permutes(weight_piece, "seq"))
    whole_tokens = gather_rows(after(token_rows, packed), "seq")
    packed = lax.all_gather(packed, "shard", axis=1)
    qkv_weight = packed[:, :, : 3 * shard_rows].reshape(
        seq_count, shard_count, 3, shard_rows, width
    )
    qkv_weight = qkv_weight.transpose(2, 0, 1, 3, 4).reshape(3, model_width, width)
    small_all = packed[:, :, 3 * shard_rows :].reshape(owner_count, -1)
    at = 0
    pieces = []
    for size in (shard_rows, shard_rows, position_bias.shape[0], router_matrix.size):
        pieces.append(small_all[:, at : at + size].reshape(-1))
        at += size
    gain_a = pieces[0].astype(F32)[None]
    gain_f = pieces[1].astype(F32)[None]
    bias_table = pieces[2].reshape(BUCKETS, head_count)
    full_router = pieces[3].reshape(model_width, experts)

    chosen = routes[0, :, 0]
    route_marks = (chosen[:, None] == jnp.arange(experts, dtype=jnp.int32)[None, :]).astype(
        jnp.int32
    )
    slot_ranks = jnp.sum((jnp.cumsum(route_marks, axis=0) - route_marks) * route_marks, axis=-1)
    slot_index = chosen * capacity + slot_ranks
    slots = experts * capacity
    place_marks = (
        slot_index[None, :] == jnp.arange(slots, dtype=jnp.int32)[:, None]
    ).astype(BF16)

    def dispatch(rows):
        placed = dot_nn(place_marks, rows).astype(BF16)
        arrived = exchange(placed.reshape(experts, capacity, model_width), group)
        return arrived.reshape(slots, model_width)

    def send_back(rows):
        back = exchange(rows.reshape(experts, capacity, model_width), group)
        return back.reshape(slots, model_width)

    output_seq = gather_rows(after(output_weight, whole_tokens), "seq")
    expert_grads = dispatch(after(grad_rows, whole_tokens, qkv_weight))
    up_full = lax.all_gather(up_weight, "rep", axis=1, tiled=True)[0]
    down_full = lax.all_gather(down_weight, "rep", axis=1, tiled=True)[0]

    bucket_marks = (
        jnp.pad(bucket_table, (0, 1), constant_values=-1)[None, :]
        == jnp.arange(BUCKETS, dtype=jnp.int32)[:, None]
    ).astype(BF16)
    own_table = lax.dynamic_slice_in_dim(bias_table, seq_place * heads, heads, 1)
    padded_heads = -(-heads // 8) * 8
    own_table = jnp.pad(own_table, ((0, 0), (0, padded_heads - heads)))
    skewed = skew_bias(dot_tn(own_table, bucket_marks), heads)

    normed_whole, qkv, probs, context_own = attention_forward(
        whole_tokens, gain_a, qkv_weight, skewed, heads, head_size
    )
    output_seq = after(output_seq, context_own)
    output_all = gather_rows(output_seq, "shard").reshape(
        shard_count, seq_count, shard_rows, model_width
    )
    output_all = output_all.transpose(1, 0, 2, 3).reshape(model_width, model_width)
    context_own = after(context_own, expert_grads)
    context = exchange(context_own.reshape(seq_count, seg_rows, width), "seq")
    context = context.transpose(1, 0, 2).reshape(seg_rows, model_width)
    inputs = token_rows.astype(F32)
    grads_out = grad_rows.astype(F32)
    middle = inputs + dot_nn(context, output_all)
    middle_inverse = inverse_rms(middle)
    normed_ffn = (middle * middle_inverse * gain_f).astype(BF16)

    expert_rows = dispatch(normed_ffn)
    owner = seq_place * shard_count + lax.axis_index("shard")
    lanes = -(-experts // TILE) * TILE
    router_lanes = jnp.pad(full_router, ((0, 0), (0, lanes - experts)))
    picked = (jnp.arange(lanes, dtype=jnp.int32) == owner).astype(F32)[None]
    up_grad, down_grad, rows_grad, gated_out, logit_grad = expert_pass(
        expert_rows, expert_grads, router_lanes, picked, up_full, down_full, experts
    )
    grad_back = send_back(rows_grad)
    router_grad = dot_tn(expert_rows, logit_grad)[:, :experts]
    normed_ffn_grad = dot_tn(place_marks, grad_back)
    up_weight_grad = lax.psum_scatter(
        up_grad[None], "rep", scatter_dimension=1, tiled=True
    ).astype(F32)
    down_weight_grad = lax.psum_scatter(
        down_grad[None], "rep", scatter_dimension=1, tiled=True
    ).astype(F32)

    gain_f_grad = jnp.sum(normed_ffn_grad * middle * middle_inverse, axis=0)
    middle_grad = grads_out + norm_backward(middle, middle_inverse, gain_f, normed_ffn_grad)
    attn_out_grad = middle_grad.astype(BF16)
    context_grad = dot_nt(attn_out_grad, output_all).astype(BF16)
    context_grad = context_grad.reshape(seg_rows, seq_count, width).transpose(1, 0, 2)
    context_grad = exchange(context_grad, "seq").reshape(length, width)
    output_grad = dot_tn(context, attn_out_grad).reshape(
        seq_count, shard_count, shard_rows, model_width
    )
    output_grad = reduce_rows(output_grad.transpose(1, 0, 2, 3), "shard")
    output_grad = reduce_rows(quarters(output_grad, rep_count), "rep")
    returned = send_back(after(gated_out, context_grad))

    qkv_grad, normed_grad_part, gain_a_grad, offset_grad = attention_backward(
        qkv, probs, context_grad, qkv_weight, whole_tokens, normed_whole, heads, head_size
    )
    output_part = reduce_rows(output_grad, "seq")
    layer_output = (middle + dot_tn(place_marks, returned)).astype(BF16)
    own_table_grad = lax.dot_general(
        bucket_marks.astype(F32),
        offset_grad,
        (((1,), (1,)), ((), ())),
        precision=lax.Precision.HIGHEST,
        preferred_element_type=F32,
    )
    table_grad = lax.dynamic_update_slice_in_dim(
        jnp.zeros((BUCKETS, head_count), F32), own_table_grad[:, :heads], seq_place * heads, 1
    )

    small_grad = jnp.concatenate(
        [
            gain_a_grad.reshape(owner_count, -1),
            gain_f_grad.reshape(owner_count, -1),
            table_grad.reshape(owner_count, -1),
            router_grad.reshape(owner_count, -1),
        ],
        axis=1,
    )
    small_grad = jnp.pad(small_grad, ((0, 0), (0, small_rows * width - small_size)))
    weight_parts = qkv_grad.reshape(3, seq_count, shard_count, shard_rows, width)
    weight_parts = weight_parts.transpose(2, 1, 0, 3, 4).reshape(
        shard_count, seq_count, 3 * shard_rows, width
    )
    small_grad = small_grad.reshape(seq_count, shard_count, small_rows, width)
    weight_parts = jnp.concatenate([weight_parts, small_grad.transpose(1, 0, 2, 3)], axis=2)
    weight_parts = reduce_rows(weight_parts, "shard")
    weight_parts = reduce_rows(quarters(weight_parts, rep_count), "rep").astype(BF16)
    weight_parts = exchange_by_permutes(
        lambda target: lax.dynamic_index_in_dim(weight_parts, target, 0, False), "seq"
    )
    weight_rows = jnp.concatenate(weight_parts, axis=1)
    normed_grad = reduce_rows(
        normed_grad_part.reshape(seq_count, seg_rows, model_width), "seq"
    )
    token_inverse = inverse_rms(inputs)
    token_input_gradient = middle_grad + norm_backward(inputs, token_inverse, gain_a, normed_grad)

    rows = jnp.concatenate([weight_rows, output_part.astype(BF16)], axis=0)
    rows = gather_rows(rows[None], "rep").astype(F32)
    part_rows = weight_rows.shape[0]
    weight_rows = rows[:, :part_rows].reshape(rep_count * part_rows, model_width)
    output_rows = rows[:, part_rows:].reshape(shard_rows, model_width)
    matrices = [weight_rows[k * shard_rows : (k + 1) * shard_rows] for k in range(3)]
    matrices.append(output_rows)
    smalls = weight_rows[3 * shard_rows :].reshape(small_rows, seq_count, width)
    smalls = jnp.sum(smalls, axis=1).reshape(-1)[:small_size]
    table_size = position_bias.shape[0]
    return (
        layer_output[None],
        token_input_gradient[None],
        smalls[:shard_rows],
        matrices[0],
        matrices[1],
        matrices[2],
        matrices[3],
        smalls[2 * shard_rows : 2 * shard_rows + table_size],
        smalls[shard_rows : 2 * shard_rows],
        smalls[2 * shard_rows + table_size :].reshape(shard_rows, experts),
        up_weight_grad,
        down_weight_grad,
    )


def solution(mesh):
    return jax.shard_map(
        per_device,
        mesh=mesh,
        in_specs=(
            P(("rep", "shard"), "seq", None),
            P(("rep", "shard"), "seq", None),
            P(("seq", "shard")),
            P(("seq", "shard"), None),
            P(("seq", "shard"), None),
            P(("seq", "shard"), None),
            P(("seq", "shard"), None),
            P(("seq", "shard")),
            P(),
            P(("seq", "shard")),
            P(("seq", "shard"), None),
            P(("rep", "shard"), "seq", None),
            P(("seq", "shard"), "rep", None),
            P(("seq", "shard"), "rep", None),
        ),
        out_specs=(
            P(("rep", "shard"), "seq", None),
            P(("rep", "shard"), "seq", None),
            P(("seq", "shard")),
            P(("seq", "shard"), None),
            P(("seq", "shard"), None),
            P(("seq", "shard"), None),
            P(("seq", "shard"), None),
            P(("seq", "shard")),
            P(("seq", "shard")),
            P(("seq", "shard"), None),
            P(("seq", "shard"), "rep", None),
            P(("seq", "shard"), "rep", None),
        ),
        check_vma=False,
    )
```

profile of v0, /device:TPU:0, one launch (start us, length us, event | category | flops | bytes accessed | tf_op | source)
XLA Modules:
  0.0 361.0 jit_solution(8221543058191588159)
XLA Ops:
  9.6 3.1 collective-permute-start
  12.7 2.6 collective-permute-start.1
  17.6 2.1 collective-permute-done
  19.7 5.8 %collective-permute-done.1 = bf16[304,192]{1,0:T(8,128)(2,1)S(1)} collective-permute-done((bf16[304,192]{1,0:T(8,128)(2,1)S(1)}, bf16[304,192]{1,0:T(8,128)(2,1)S(1)}, u32[]{:S(2)}, u32[]{:S(2)}) %collective-permute-start.1) | collective-permute-done | bytes 116768 | tf_op jit(solution)/shard_map/ppermute | solution.py:380
  26.6 3.8 %collective-permute-start.3 = (bf16[256,768]{1,0:T(8,128)(2,1)S(1)}, bf16[256,768]{1,0:T(8,128)(2,1)S(1)}, u32[]{:S(2)}, u32[]{:S(2)}) collective-permute-start(bf16[256,768]{1,0:T(8,128)(2,1)S(1)} %bitcast.204), channel_id=1, source_target_pairs={{0,2},{2,4},{4,6},{6,0},{1,3},{3,5},{5,7},{7,1},{8,10},{10,12},{12... | collective-permute-start | bytes 1179656 | tf_op jit(solution)/shard_map/ppermute | solution.py:353
  30.4 1.6 collective-permute-start.4
  32.8 2.7 all-gather
  38.6 3.1 collective-permute-done.3
  42.5 14.3 %collective-permute-done.4 = bf16[256,768]{1,0:T(8,128)(2,1)S(1)} collective-permute-done((bf16[256,768]{1,0:T(8,128)(2,1)S(1)}, bf16[256,768]{1,0:T(8,128)(2,1)S(1)}, u32[]{:S(2)}, u32[]{:S(2)}) %collective-permute-start.4) | collective-permute-done | bytes 393248 | tf_op jit(solution)/shard_map/ppermute | solution.py:353
  59.6 12.0 %all-to-all-start = ((bf16[8,64,768]{2,1,0:T(8,128)(2,1)}), bf16[8,64,768]{2,1,0:T(8,128)(2,1)S(1)}, u32[]{:S(2)}, u32[]{:S(2)}) async-start(bf16[8,64,768]{2,1,0:T(8,128)(2,1)} %bitcast.14), calls=%async_computation | async-start | bytes 1572864 | tf_op jit(solution)/shard_map/all_to_all | solution.py:401
  73.0 2.0 shard_map.229.skewed_ref
  75.0 1.7 copy-done
  76.8 2.1 collective-permute-start.6
  78.9 2.4 collective-permute-start.7
  81.2 1.5 collective-permute-start.8
  82.7 13.4 %shard_map.230 = (bf16[1024,768]{1,0:T(8,128)(2,1)S(1)}, bf16[3,1024,192]{2,1,0:T(8,128)(2,1)S(1)}, bf16[3,1024,1024]{2,1,0:T(8,128)(2,1)}, bf16[1024,192]{1,0:T(8,128)(2,1)S(1)}) custom-call(bf16[1024,768]{1,0:T(8,128)(2,1)} %constant_dynamic-update-slice_fusion.10.tokens_ref, f32[1,768]{1,0:T(1,128)S(1)} %reshape.295.gain_ref, ...), custom_call_target="tpu_custom_call" | custom-call | flops 1711276032 | bytes 16777216 | tf_op jit(solution)/shard_map/pallas_call | solution.py:96
  100.6 1.9 collective-permute-done.7
  104.8 5.3 %all-to-all-start.1 = ((bf16[4,256,192]{1,2,0:T(8,128)(2,1)}), bf16[4,256,192]{1,2,0:T(8,128)(2,1)S(1)}, u32[]{:S(2)}, u32[]{:S(2)}) async-start(bf16[4,256,192]{1,2,0:T(8,128)(2,1)} %copy.80), calls=%async_computation.1 | async-start | bytes 786432 | tf_op jit(solution)/shard_map/all_to_all | solution.py:401
  113.6 8.8 %all-to-all-done.1 = bf16[4,256,192]{1,2,0:T(8,128)(2,1)S(1)} async-done(((bf16[4,256,192]{1,2,0:T(8,128)(2,1)}), bf16[4,256,192]{1,2,0:T(8,128)(2,1)S(1)}, u32[]{:S(2)}, u32[]{:S(2)}) %all-to-all-start.1) | async-done | bytes 393248 | tf_op jit(solution)/shard_map/all_to_all | solution.py:401
  122.4 1.9 multiply_reduce_fusion.2
  126.5 3.5 all-to-all-start.2
  132.3 18.6 %all-to-all-done.2 = bf16[8,64,768]{2,1,0:T(8,128)(2,1)S(1)} async-done(((bf16[8,64,768]{2,1,0:T(8,128)(2,1)}), bf16[8,64,768]{2,1,0:T(8,128)(2,1)S(1)}, u32[]{:S(2)}, u32[]{:S(2)}) %all-to-all-start.2) | async-done | bytes 786464 | tf_op jit(solution)/shard_map/all_to_all | solution.py:401
  151.0 21.8 %shard_map.231 = (bf16[3072,768]{1,0:T(8,128)(2,1)}, bf16[3072,768]{1,0:T(8,128)(2,1)}, bf16[512,768]{1,0:T(8,128)(2,1)}, bf16[512,768]{1,0:T(8,128)(2,1)}, bf16[512,128]{1,0:T(8,128)(2,1)S(1)}) custom-call(bf16[512,768]{1,0:T(8,128)(2,1)S(1)} %bitcast.192, bf16[512,768]{1,0:T(8,128)(2,1)S(1)} %bitcast.198, bf16[768,128]{1,0:T(8,128)(2,1)S(1)} %pad.23.router_ref, ...), custom_call_target="tpu_custom_call" | custom-call | flops 14495514624 | bytes 16777216 | tf_op jit(solution)/shard_map/pallas_call | solution.py:295
  173.4 4.4 %all-to-all-start.3 = ((bf16[8,64,768]{2,1,0:T(8,128)(2,1)}), bf16[8,64,768]{2,1,0:T(8,128)(2,1)}, u32[]{:S(2)}, u32[]{:S(2)}) async-start(bf16[8,64,768]{2,1,0:T(8,128)(2,1)} %bitcast.26), calls=%async_computation.3 | async-start | bytes 1572864 | tf_op jit(solution)/shard_map/all_to_all | solution.py:401
  177.9 20.8 %all-to-all-done.3 = bf16[8,64,768]{2,1,0:T(8,128)(2,1)} async-done(((bf16[8,64,768]{2,1,0:T(8,128)(2,1)}), bf16[8,64,768]{2,1,0:T(8,128)(2,1)}, u32[]{:S(2)}, u32[]{:S(2)}) %all-to-all-start.3) | async-done | bytes 786464 | tf_op jit(solution)/shard_map/all_to_all | solution.py:401
  198.8 1.7 multiply_reduce_fusion
  203.6 4.2 %all-to-all-start.4 = ((bf16[4,256,192]{1,2,0:T(8,128)(2,1)}), bf16[4,256,192]{1,2,0:T(8,128)(2,1)}, u32[]{:S(2)}, u32[]{:S(2)}) async-start(bf16[4,256,192]{1,2,0:T(8,128)(2,1)} %bitcast.221), calls=%async_computation.4 | async-start | bytes 786432 | tf_op jit(solution)/shard_map/all_to_all | solution.py:401
  210.7 1.4 copy-done.12
  213.0 6.6 %all-to-all-done.4 = bf16[4,256,192]{1,2,0:T(8,128)(2,1)} async-done(((bf16[4,256,192]{1,2,0:T(8,128)(2,1)}), bf16[4,256,192]{1,2,0:T(8,128)(2,1)}, u32[]{:S(2)}, u32[]{:S(2)}) %all-to-all-start.4) | async-done | bytes 393248 | tf_op jit(solution)/shard_map/all_to_all | solution.py:401
  220.9 1.4 copy-done.3
  222.3 16.9 %shard_map.232 = (f32[3,768,192]{2,1,0:T(8,128)}, bf16[1024,768]{1,0:T(8,128)(2,1)S(1)}, f32[1,768]{1,0:T(1,128)S(1)}, f32[8,2048]{1,0:T(8,128)S(1)}) custom-call(bf16[3,1024,192]{2,1,0:T(8,128)(2,1)S(1)} %copy-done.3, bf16[3,1024,1024]{2,1,0:T(8,128)(2,1)} %get-tuple-element.41.probs_ref, bf16[1024,192]{1,0:T(8,128)(2,1)S(1)} %bitcast.197, ...), custom_call_target="tpu_custom_call" | custom-call | flops 3422552064 | bytes 16777216 | tf_op jit(solution)/shard_map/pallas_call | solution.py:199
  240.1 2.0 copy.84
  242.4 1.6 bitcast_add_fusion
  244.9 1.6 collective-permute-start.21
  246.5 1.5 collective-permute-start.22
  248.0 1.4 collective-permute-start.23
  250.6 2.4 fusion.3
  253.0 2.9 collective-permute-done.21
  255.9 2.4 collective-permute-done.22
  258.4 3.4 collective-permute-done.23
  264.2 2.2 collective-permute-start.25
  266.4 1.6 collective-permute-start.26
  269.1 1.7 copy.88
  271.5 4.5 %all-to-all-start.5 = ((bf16[8,64,768]{2,1,0:T(8,128)(2,1)}), bf16[8,64,768]{2,1,0:T(8,128)(2,1)}, u32[]{:S(2)}, u32[]{:S(2)}) async-start(bf16[8,64,768]{2,1,0:T(8,128)(2,1)} %bitcast.31), calls=%async_computation.5 | async-start | bytes 1572864 | tf_op jit(solution)/shard_map/all_to_all | solution.py:401
  276.6 2.9 collective-permute-start.11
  279.5 1.5 collective-permute-start.12
  281.0 1.6 fusion.45
  282.6 2.2 bitcast_add_fusion.1
  284.8 2.8 copy.90
  287.6 2.4 reshape.289
  291.2 1.5 collective-permute-start.14
  294.6 20.8 %collective-permute-done.11 = bf16[256,768]{1,0:T(8,128)(2,1)S(1)} collective-permute-done((bf16[256,768]{1,0:T(8,128)(2,1)}, bf16[256,768]{1,0:T(8,128)(2,1)S(1)}, u32[]{:S(2)}, u32[]{:S(2)}) %collective-permute-start.11) | collective-permute-done | bytes 393248 | tf_op jit(solution)/shard_map/ppermute | solution.py:365
  315.5 1.6 fusion.5
  318.3 8.9 %collective-permute-start.17 = (bf16[76,192]{1,0:T(8,128)(2,1)S(1)}, bf16[76,192]{1,0:T(8,128)(2,1)S(1)}, u32[]{:S(2)}, u32[]{:S(2)}) collective-permute-start(bf16[76,192]{1,0:T(8,128)(2,1)S(1)} %get-tuple-element.132), channel_id=1, source_target_pairs={{0,2},{2,4},{4,6},{6,0},{1,3},{3,5},{5,7},{7,1},{8,10},{10,12},{12... | collective-permute-start | bytes 87560 | tf_op jit(solution)/shard_map/ppermute | solution.py:380
  328.2 1.5 collective-permute-start.19
  329.7 2.9 collective-permute-done.18
  332.8 1.4 collective-permute-start.27
  334.8 2.2 fusion.9
  337.1 1.4 collective-permute-start.29
  338.5 1.4 collective-permute-done.27
  339.9 1.7 collective-permute-done.28
  346.4 2.3 fusion.4
  348.7 2.8 convert_element_type.268
  351.6 2.8 convert_element_type.269
  (219 shorter events, 56.8 us)
Async XLA Ops:
  7.2 1.8 copy-start.37
  7.2 1.8 copy-start.35
  7.2 1.8 copy-start.36
  7.2 2.0 copy-start.25
  7.2 2.0 copy-start.26
  7.2 2.0 copy-start.27
  7.2 143.7 %all-gather.4.cloned.1.call-start = ((), (), s32[]{:S(2)}) async-start(), calls=%async_computation.8 | async-start | bytes 5898240 | tf_op jit(solution)/shard_map/all_gather | solution.py:492
  8.0 143.0 %all-gather.6.cloned.1.call-start = ((), (), s32[]{:S(2)}) async-start(), calls=%async_computation.9 | async-start | bytes 5898240 | tf_op jit(solution)/shard_map/all_gather | solution.py:493
  9.2 7.5 %copy-start.32 = (s32[1,256,1]{1,2,0:T(1,128)S(1)}, s32[1,256,1]{1,2,0:T(1,128)}, u32[]{:S(2)}) copy-start(s32[1,256,1]{1,2,0:T(1,128)} %param.25) | copy-start | bytes 3076
  9.6 10.1 %collective-permute-start = (bf16[304,192]{1,0:T(8,128)(2,1)S(1)}, bf16[304,192]{1,0:T(8,128)(2,1)S(1)}, u32[]{:S(2)}, u32[]{:S(2)}) collective-permute-start(bf16[304,192]{1,0:T(8,128)(2,1)S(1)} %get-tuple-element.137), channel_id=1, source_target_pairs={{0,2},{2,4},{4,6},{6,0},{1,3},{3,5},{5,7},{7,1},{8,10},{10,12},{12... | collective-permute-start | bytes 350216 | tf_op jit(solution)/shard_map/ppermute | solution.py:380
  12.7 12.8 %collective-permute-start.1 = (bf16[304,192]{1,0:T(8,128)(2,1)S(1)}, bf16[304,192]{1,0:T(8,128)(2,1)S(1)}, u32[]{:S(2)}, u32[]{:S(2)}) collective-permute-start(bf16[304,192]{1,0:T(8,128)(2,1)S(1)} %get-tuple-element.138), channel_id=1, source_target_pairs={{0,4},{2,6},{4,0},{6,2},{1,5},{3,7},{5,1},{7,3},{8,12},{10,14},{12... | collective-permute-start | bytes 350216 | tf_op jit(solution)/shard_map/ppermute | solution.py:380
  15.3 10.2 %collective-permute-start.2 = (bf16[304,192]{1,0:T(8,128)(2,1)S(1)}, bf16[304,192]{1,0:T(8,128)(2,1)S(1)}, u32[]{:S(2)}, u32[]{:S(2)}) collective-permute-start(bf16[304,192]{1,0:T(8,128)(2,1)S(1)} %get-tuple-element.139), channel_id=1, source_target_pairs={{0,6},{2,0},{4,2},{6,4},{1,7},{3,1},{5,3},{7,5},{8,14},{10,8},{12,... | collective-permute-start | bytes 350216 | tf_op jit(solution)/shard_map/ppermute | solution.py:380
  26.6 15.0 %collective-permute-start.3 = (bf16[256,768]{1,0:T(8,128)(2,1)S(1)}, bf16[256,768]{1,0:T(8,128)(2,1)S(1)}, u32[]{:S(2)}, u32[]{:S(2)}) collective-permute-start(bf16[256,768]{1,0:T(8,128)(2,1)S(1)} %bitcast.204), channel_id=1, source_target_pairs={{0,2},{2,4},{4,6},{6,0},{1,3},{3,5},{5,7},{7,1},{8,10},{10,12},{12... | collective-permute-start | bytes 1179656 | tf_op jit(solution)/shard_map/ppermute | solution.py:353
  30.4 26.3 %collective-permute-start.4 = (bf16[256,768]{1,0:T(8,128)(2,1)S(1)}, bf16[256,768]{1,0:T(8,128)(2,1)S(1)}, u32[]{:S(2)}, u32[]{:S(2)}) collective-permute-start(bf16[256,768]{1,0:T(8,128)(2,1)S(1)} %bitcast.205), channel_id=1, source_target_pairs={{0,4},{2,6},{4,0},{6,2},{1,5},{3,7},{5,1},{7,3},{8,12},{10,14},{12... | collective-permute-start | bytes 1179656 | tf_op jit(solution)/shard_map/ppermute | solution.py:353
  32.1 25.4 %collective-permute-start.5 = (bf16[256,768]{1,0:T(8,128)(2,1)S(1)}, bf16[256,768]{1,0:T(8,128)(2,1)S(1)}, u32[]{:S(2)}, u32[]{:S(2)}) collective-permute-start(bf16[256,768]{1,0:T(8,128)(2,1)S(1)} %bitcast.206), channel_id=1, source_target_pairs={{0,6},{2,0},{4,2},{6,4},{1,7},{3,1},{5,3},{7,5},{8,14},{10,8},{12,... | collective-permute-start | bytes 1179656 | tf_op jit(solution)/shard_map/ppermute | solution.py:353
  38.6 19.7 %copy-start.17 = (bf16[1,256,768]{2,1,0:T(8,128)(2,1)S(1)}, bf16[1,256,768]{2,1,0:T(8,128)(2,1)}, u32[]{:S(2)}) copy-start(bf16[1,256,768]{2,1,0:T(8,128)(2,1)} %param.15) | copy-start | bytes 1179652
  58.3 13.3 %copy-start.33 = (s32[2047]{0:T(1024)S(1)}, s32[2047]{0:T(1024)}, u32[]{:S(2)}) copy-start(s32[2047]{0:T(1024)} %param.22) | copy-start | bytes 24568
  59.6 44.3 %all-to-all-start = ((bf16[8,64,768]{2,1,0:T(8,128)(2,1)}), bf16[8,64,768]{2,1,0:T(8,128)(2,1)S(1)}, u32[]{:S(2)}, u32[]{:S(2)}) async-start(bf16[8,64,768]{2,1,0:T(8,128)(2,1)} %bitcast.14), calls=%async_computation | async-start | bytes 1572864 | tf_op jit(solution)/shard_map/all_to_all | solution.py:401
  73.0 3.8 %copy-start.28 = (bf16[96,768]{1,0:T(8,128)(2,1)S(1)}, bf16[96,768]{1,0:T(8,128)(2,1)}, u32[]{:S(2)}) copy-start(bf16[96,768]{1,0:T(8,128)(2,1)} %param.20) | copy-start | bytes 442372
  76.8 23.1 %collective-permute-start.6 = (bf16[96,768]{1,0:T(8,128)(2,1)S(1)}, bf16[96,768]{1,0:T(8,128)(2,1)S(1)}, u32[]{:S(2)}, u32[]{:S(2)}) collective-permute-start(bf16[96,768]{1,0:T(8,128)(2,1)S(1)} %copy-done.28), channel_id=1, source_target_pairs={{0,2},{2,4},{4,6},{6,0},{1,3},{3,5},{5,7},{7,1},{8,10},{10,12},{12... | collective-permute-start | bytes 442376 | tf_op jit(solution)/shard_map/ppermute | solution.py:353
  78.9 23.6 %collective-permute-start.7 = (bf16[96,768]{1,0:T(8,128)(2,1)S(1)}, bf16[96,768]{1,0:T(8,128)(2,1)S(1)}, u32[]{:S(2)}, u32[]{:S(2)}) collective-permute-start(bf16[96,768]{1,0:T(8,128)(2,1)S(1)} %copy-done.28), channel_id=1, source_target_pairs={{0,4},{2,6},{4,0},{6,2},{1,5},{3,7},{5,1},{7,3},{8,12},{10,14},{12... | collective-permute-start | bytes 442376 | tf_op jit(solution)/shard_map/ppermute | solution.py:353
  81.2 21.9 %collective-permute-start.8 = (bf16[96,768]{1,0:T(8,128)(2,1)S(1)}, bf16[96,768]{1,0:T(8,128)(2,1)S(1)}, u32[]{:S(2)}, u32[]{:S(2)}) collective-permute-start(bf16[96,768]{1,0:T(8,128)(2,1)S(1)} %copy-done.28), channel_id=1, source_target_pairs={{0,6},{2,0},{4,2},{6,4},{1,7},{3,1},{5,3},{7,5},{8,14},{10,8},{12,... | collective-permute-start | bytes 442376 | tf_op jit(solution)/shard_map/ppermute | solution.py:353
  103.8 7.5 %collective-permute-start.9 = (bf16[384,768]{1,0:T(8,128)(2,1)}, bf16[384,768]{1,0:T(8,128)(2,1)}, u32[]{:S(2)}, u32[]{:S(2)}) collective-permute-start(bf16[384,768]{1,0:T(8,128)(2,1)} %constant_dynamic-update-slice_fusion.6), channel_id=1, source_target_pairs={{0,1},{1,0},{2,3},{3,2},{4,5},{5,4},{6,7},{7,6},{8,9},{9,8},{10,11... | collective-permute-start | bytes 1769480 | tf_op jit(solution)/shard_map/ppermute | solution.py:353
  104.8 17.6 %all-to-all-start.1 = ((bf16[4,256,192]{1,2,0:T(8,128)(2,1)}), bf16[4,256,192]{1,2,0:T(8,128)(2,1)S(1)}, u32[]{:S(2)}, u32[]{:S(2)}) async-start(bf16[4,256,192]{1,2,0:T(8,128)(2,1)} %copy.80), calls=%async_computation.1 | async-start | bytes 786432 | tf_op jit(solution)/shard_map/all_to_all | solution.py:401
  124.2 2.3 copy-start.30
  126.5 24.5 %all-to-all-start.2 = ((bf16[8,64,768]{2,1,0:T(8,128)(2,1)}), bf16[8,64,768]{2,1,0:T(8,128)(2,1)S(1)}, u32[]{:S(2)}, u32[]{:S(2)}) async-start(bf16[8,64,768]{2,1,0:T(8,128)(2,1)} %bitcast.216), calls=%async_computation.2 | async-start | bytes 1572864 | tf_op jit(solution)/shard_map/all_to_all | solution.py:401
  130.1 218.6 %reduce-scatter.3.cloned.1.call-start = ((), (), s32[]{:S(2)}) async-start(), calls=%async_computation.10 | async-start | bytes 5898240 | tf_op jit(solution)/shard_map/reduce_scatter | solution.py:532
  172.8 178.8 %reduce-scatter.5.cloned.1.call-start = ((), (), s32[]{:S(2)}) async-start(), calls=%async_computation.11 | async-start | bytes 5898240 | tf_op jit(solution)/shard_map/reduce_scatter | solution.py:535
  173.4 25.4 %copy-start.6 = (f32[256,768]{1,0:T(8,128)S(1)}, f32[256,768]{1,0:T(8,128)}, u32[]{:S(2)}) copy-start(f32[256,768]{1,0:T(8,128)} %copy-done.5) | copy-start | bytes 2359300
  173.4 25.3 %all-to-all-start.3 = ((bf16[8,64,768]{2,1,0:T(8,128)(2,1)}), bf16[8,64,768]{2,1,0:T(8,128)(2,1)}, u32[]{:S(2)}, u32[]{:S(2)}) async-start(bf16[8,64,768]{2,1,0:T(8,128)(2,1)} %bitcast.26), calls=%async_computation.3 | async-start | bytes 1572864 | tf_op jit(solution)/shard_map/all_to_all | solution.py:401
  177.8 22.7 %copy-start.31 = (f32[256]{0:T(256)S(1)}, f32[256]{0:T(256)}, u32[]{:S(2)}) copy-start(f32[256]{0:T(256)} %copy-done.30) | copy-start | bytes 3076
  203.6 6.7 %copy-start.9 = (f32[256,768]{1,0:T(8,128)S(1)}, f32[256,768]{1,0:T(8,128)}, u32[]{:S(2)}) copy-start(f32[256,768]{1,0:T(8,128)} %copy-done.8) | copy-start | bytes 2359300
  203.6 16.1 %all-to-all-start.4 = ((bf16[4,256,192]{1,2,0:T(8,128)(2,1)}), bf16[4,256,192]{1,2,0:T(8,128)(2,1)}, u32[]{:S(2)}, u32[]{:S(2)}) async-start(bf16[4,256,192]{1,2,0:T(8,128)(2,1)} %bitcast.221), calls=%async_computation.4 | async-start | bytes 786432 | tf_op jit(solution)/shard_map/all_to_all | solution.py:401
  213.0 29.0 %collective-permute-start.20 = (bf16[4,96,768]{2,1,0:T(8,128)(2,1)}, bf16[4,96,768]{2,1,0:T(8,128)(2,1)}, u32[]{:S(2)}, u32[]{:S(2)}) collective-permute-start(bf16[4,96,768]{2,1,0:T(8,128)(2,1)} %fusion.14), channel_id=1, source_target_pairs={{0,1},{1,0},{2,3},{3,2},{4,5},{5,4},{6,7},{7,6},{8,9},{9,8},{10,11... | collective-permute-start | bytes 1769480 | tf_op jit(solution)/shard_map/ppermute | solution.py:365
  240.1 2.4 copy-start.13
  242.1 7.4 %copy-start.4 = (f32[3,4,2,96,192]{4,3,0,1,2:T(8,128)}, f32[3,4,2,96,192]{4,3,0,1,2:T(8,128)S(1)}, u32[]{:S(2)}) copy-start(f32[3,4,2,96,192]{4,3,0,1,2:T(8,128)S(1)} %copy.84) | copy-start | bytes 5308420
  244.9 11.1 %collective-permute-start.21 = (bf16[4,24,768]{2,1,0:T(8,128)(2,1)}, bf16[4,24,768]{2,1,0:T(8,128)(2,1)}, u32[]{:S(2)}, u32[]{:S(2)}) collective-permute-start(bf16[4,24,768]{2,1,0:T(8,128)(2,1)} %get-tuple-element.110), channel_id=1, source_target_pairs={{0,8},{8,16},{16,24},{24,0},{1,9},{9,17},{17,25},{25,1},{2,10},{10... | collective-permute-start | bytes 442376 | tf_op jit(solution)/shard_map/ppermute | solution.py:365
  246.5 11.9 %collective-permute-start.22 = (bf16[4,24,768]{2,1,0:T(8,128)(2,1)}, bf16[4,24,768]{2,1,0:T(8,128)(2,1)}, u32[]{:S(2)}, u32[]{:S(2)}) collective-permute-start(bf16[4,24,768]{2,1,0:T(8,128)(2,1)} %get-tuple-element.111), channel_id=1, source_target_pairs={{0,16},{8,24},{16,0},{24,8},{1,17},{9,25},{17,1},{25,9},{2,18},{10... | collective-permute-start | bytes 442376 | tf_op jit(solution)/shard_map/ppermute | solution.py:365
  248.0 13.8 %collective-permute-start.23 = (bf16[4,24,768]{2,1,0:T(8,128)(2,1)}, bf16[4,24,768]{2,1,0:T(8,128)(2,1)}, u32[]{:S(2)}, u32[]{:S(2)}) collective-permute-start(bf16[4,24,768]{2,1,0:T(8,128)(2,1)} %get-tuple-element.112), channel_id=1, source_target_pairs={{0,24},{8,0},{16,8},{24,16},{1,25},{9,1},{17,9},{25,17},{2,26},{10... | collective-permute-start | bytes 442376 | tf_op jit(solution)/shard_map/ppermute | solution.py:365
  250.6 32.0 %collective-permute-start.13 = (bf16[4,304,192]{1,2,0:T(8,128)(2,1)}, bf16[4,304,192]{1,2,0:T(8,128)(2,1)}, u32[]{:S(2)}, u32[]{:S(2)}) collective-permute-start(bf16[4,304,192]{1,2,0:T(8,128)(2,1)} %copy.89), channel_id=1, source_target_pairs={{0,1},{1,0},{2,3},{3,2},{4,5},{5,4},{6,7},{7,6},{8,9},{9,8},{10,11... | collective-permute-start | bytes 1400840 | tf_op jit(solution)/shard_map/ppermute | solution.py:365
  264.2 11.7 %collective-permute-start.24 = (bf16[24,768]{1,0:T(8,128)(2,1)S(1)}, bf16[24,768]{1,0:T(8,128)(2,1)S(1)}, u32[]{:S(2)}, u32[]{:S(2)}) collective-permute-start(bf16[24,768]{1,0:T(8,128)(2,1)S(1)} %get-tuple-element.123), channel_id=1, source_target_pairs={{0,2},{2,4},{4,6},{6,0},{1,3},{3,5},{5,7},{7,1},{8,10},{10,12},{12... | collective-permute-start | bytes 110600 | tf_op jit(solution)/shard_map/ppermute | solution.py:365
  264.2 15.3 %collective-permute-start.25 = (bf16[24,768]{1,0:T(8,128)(2,1)}, bf16[24,768]{1,0:T(8,128)(2,1)}, u32[]{:S(2)}, u32[]{:S(2)}) collective-permute-start(bf16[24,768]{1,0:T(8,128)(2,1)} %get-tuple-element.125), channel_id=1, source_target_pairs={{0,4},{2,6},{4,0},{6,2},{1,5},{3,7},{5,1},{7,3},{8,12},{10,14},{12... | collective-permute-start | bytes 110600 | tf_op jit(solution)/shard_map/ppermute | solution.py:365
  266.4 14.6 %collective-permute-start.26 = (bf16[24,768]{1,0:T(8,128)(2,1)}, bf16[24,768]{1,0:T(8,128)(2,1)}, u32[]{:S(2)}, u32[]{:S(2)}) collective-permute-start(bf16[24,768]{1,0:T(8,128)(2,1)} %get-tuple-element.124), channel_id=1, source_target_pairs={{0,6},{2,0},{4,2},{6,4},{1,7},{3,1},{5,3},{7,5},{8,14},{10,8},{12,... | collective-permute-start | bytes 110600 | tf_op jit(solution)/shard_map/ppermute | solution.py:365
  270.8 22.5 %collective-permute-start.10 = (bf16[256,768]{1,0:T(8,128)(2,1)}, bf16[256,768]{1,0:T(8,128)(2,1)S(1)}, u32[]{:S(2)}, u32[]{:S(2)}) collective-permute-start(bf16[256,768]{1,0:T(8,128)(2,1)} %get-tuple-element.104), channel_id=1, source_target_pairs={{0,2},{2,4},{4,6},{6,0},{1,3},{3,5},{5,7},{7,1},{8,10},{10,12},{12... | collective-permute-start | bytes 1179656 | tf_op jit(solution)/shard_map/ppermute | solution.py:365
  271.5 75.0 %all-to-all-start.5 = ((bf16[8,64,768]{2,1,0:T(8,128)(2,1)}), bf16[8,64,768]{2,1,0:T(8,128)(2,1)}, u32[]{:S(2)}, u32[]{:S(2)}) async-start(bf16[8,64,768]{2,1,0:T(8,128)(2,1)} %bitcast.31), calls=%async_computation.5 | async-start | bytes 1572864 | tf_op jit(solution)/shard_map/all_to_all | solution.py:401
  276.6 38.8 %collective-permute-start.11 = (bf16[256,768]{1,0:T(8,128)(2,1)}, bf16[256,768]{1,0:T(8,128)(2,1)S(1)}, u32[]{:S(2)}, u32[]{:S(2)}) collective-permute-start(bf16[256,768]{1,0:T(8,128)(2,1)} %get-tuple-element.106), channel_id=1, source_target_pairs={{0,4},{2,6},{4,0},{6,2},{1,5},{3,7},{5,1},{7,3},{8,12},{10,14},{12... | collective-permute-start | bytes 1179656 | tf_op jit(solution)/shard_map/ppermute | solution.py:365
  279.5 35.9 %collective-permute-start.12 = (bf16[256,768]{1,0:T(8,128)(2,1)}, bf16[256,768]{1,0:T(8,128)(2,1)}, u32[]{:S(2)}, u32[]{:S(2)}) collective-permute-start(bf16[256,768]{1,0:T(8,128)(2,1)} %get-tuple-element.105), channel_id=1, source_target_pairs={{0,6},{2,0},{4,2},{6,4},{1,7},{3,1},{5,3},{7,5},{8,14},{10,8},{12,... | collective-permute-start | bytes 1179656 | tf_op jit(solution)/shard_map/ppermute | solution.py:365
  287.6 27.9 %copy-start.15 = (bf16[1,256,768]{2,1,0:T(8,128)(2,1)S(1)}, bf16[1,256,768]{2,1,0:T(8,128)(2,1)}, u32[]{:S(2)}) copy-start(bf16[1,256,768]{2,1,0:T(8,128)(2,1)} %param.14) | copy-start | bytes 1179652
  291.2 25.8 %collective-permute-start.14 = (bf16[4,76,192]{2,1,0:T(8,128)(2,1)S(1)}, bf16[4,76,192]{2,1,0:T(8,128)(2,1)S(1)}, u32[]{:S(2)}, u32[]{:S(2)}) collective-permute-start(bf16[4,76,192]{2,1,0:T(8,128)(2,1)S(1)} %get-tuple-element.107), channel_id=1, source_target_pairs={{0,8},{8,16},{16,24},{24,0},{1,9},{9,17},{17,25},{25,1},{2,10},{10... | collective-permute-start | bytes 350216 | tf_op jit(solution)/shard_map/ppermute | solution.py:365
  292.8 24.3 %collective-permute-start.15 = (bf16[4,76,192]{2,1,0:T(8,128)(2,1)S(1)}, bf16[4,76,192]{2,1,0:T(8,128)(2,1)S(1)}, u32[]{:S(2)}, u32[]{:S(2)}) collective-permute-start(bf16[4,76,192]{2,1,0:T(8,128)(2,1)S(1)} %get-tuple-element.109), channel_id=1, source_target_pairs={{0,16},{8,24},{16,0},{24,8},{1,17},{9,25},{17,1},{25,9},{2,18},{10... | collective-permute-start | bytes 350216 | tf_op jit(solution)/shard_map/ppermute | solution.py:365
  293.3 24.9 %copy-start.19 = (bf16[256,768]{1,0:T(8,128)(2,1)}, bf16[256,768]{1,0:T(8,128)(2,1)S(1)}, u32[]{:S(2)}) copy-start(bf16[256,768]{1,0:T(8,128)(2,1)S(1)} %collective-permute-done.10) | copy-start | bytes 1179652
  293.3 23.8 %collective-permute-start.16 = (bf16[4,76,192]{2,1,0:T(8,128)(2,1)S(1)}, bf16[4,76,192]{2,1,0:T(8,128)(2,1)S(1)}, u32[]{:S(2)}, u32[]{:S(2)}) collective-permute-start(bf16[4,76,192]{2,1,0:T(8,128)(2,1)S(1)} %get-tuple-element.108), channel_id=1, source_target_pairs={{0,24},{8,0},{16,8},{24,16},{1,25},{9,1},{17,9},{25,17},{2,26},{10... | collective-permute-start | bytes 350216 | tf_op jit(solution)/shard_map/ppermute | solution.py:365
  315.5 2.8 copy-start.21
  317.0 15.7 %copy-start.24 = (bf16[24,768]{1,0:T(8,128)(2,1)S(1)}, bf16[24,768]{1,0:T(8,128)(2,1)}, u32[]{:S(2)}) copy-start(bf16[24,768]{1,0:T(8,128)(2,1)} %fusion.45) | copy-start | bytes 110596
  317.0 17.8 %copy-start.10 = (f32[256,768]{1,0:T(8,128)S(1)}, f32[256,768]{1,0:T(8,128)}, u32[]{:S(2)}) copy-start(f32[256,768]{1,0:T(8,128)} %copy-done.8) | copy-start | bytes 2359300
  318.3 16.6 %copy-start.20 = (bf16[256,768]{1,0:T(8,128)(2,1)S(1)}, bf16[256,768]{1,0:T(8,128)(2,1)}, u32[]{:S(2)}) copy-start(bf16[256,768]{1,0:T(8,128)(2,1)} %copy-done.19) | copy-start | bytes 1179652
  318.3 16.6 %copy-start.22 = (bf16[256,768]{1,0:T(8,128)(2,1)S(1)}, bf16[256,768]{1,0:T(8,128)(2,1)}, u32[]{:S(2)}) copy-start(bf16[256,768]{1,0:T(8,128)(2,1)} %copy-done.21) | copy-start | bytes 1179652
  318.3 11.4 %collective-permute-start.17 = (bf16[76,192]{1,0:T(8,128)(2,1)S(1)}, bf16[76,192]{1,0:T(8,128)(2,1)S(1)}, u32[]{:S(2)}, u32[]{:S(2)}) collective-permute-start(bf16[76,192]{1,0:T(8,128)(2,1)S(1)} %get-tuple-element.132), channel_id=1, source_target_pairs={{0,2},{2,4},{4,6},{6,0},{1,3},{3,5},{5,7},{7,1},{8,10},{10,12},{12... | collective-permute-start | bytes 87560 | tf_op jit(solution)/shard_map/ppermute | solution.py:380
  327.2 5.4 %collective-permute-start.18 = (bf16[76,192]{1,0:T(8,128)(2,1)S(1)}, bf16[76,192]{1,0:T(8,128)(2,1)S(1)}, u32[]{:S(2)}, u32[]{:S(2)}) collective-permute-start(bf16[76,192]{1,0:T(8,128)(2,1)S(1)} %get-tuple-element.131), channel_id=1, source_target_pairs={{0,4},{2,6},{4,0},{6,2},{1,5},{3,7},{5,1},{7,3},{8,12},{10,14},{12... | collective-permute-start | bytes 87560 | tf_op jit(solution)/shard_map/ppermute | solution.py:380
  328.2 4.4 %collective-permute-start.19 = (bf16[76,192]{1,0:T(8,128)(2,1)S(1)}, bf16[76,192]{1,0:T(8,128)(2,1)S(1)}, u32[]{:S(2)}, u32[]{:S(2)}) collective-permute-start(bf16[76,192]{1,0:T(8,128)(2,1)S(1)} %get-tuple-element.130), channel_id=1, source_target_pairs={{0,6},{2,0},{4,2},{6,4},{1,7},{3,1},{5,3},{7,5},{8,14},{10,8},{12,... | collective-permute-start | bytes 87560 | tf_op jit(solution)/shard_map/ppermute | solution.py:380
  332.8 7.0 %collective-permute-start.27 = (bf16[1,100,768]{2,1,0:T(8,128)(2,1)S(1)}, bf16[1,100,768]{2,1,0:T(8,128)(2,1)S(1)}, u32[]{:S(2)}, u32[]{:S(2)}) collective-permute-start(bf16[1,100,768]{2,1,0:T(8,128)(2,1)S(1)} %get-tuple-element.103), channel_id=1, source_target_pairs={{0,8},{8,16},{16,24},{24,0},{1,9},{9,17},{17,25},{25,1},{2,10},{10... | collective-permute-start | bytes 460808 | tf_op jit(solution)/shard_map/ppermute | solution.py:353
  334.2 7.4 %collective-permute-start.28 = (bf16[1,100,768]{2,1,0:T(8,128)(2,1)S(1)}, bf16[1,100,768]{2,1,0:T(8,128)(2,1)S(1)}, u32[]{:S(2)}, u32[]{:S(2)}) collective-permute-start(bf16[1,100,768]{2,1,0:T(8,128)(2,1)S(1)} %get-tuple-element.103), channel_id=1, source_target_pairs={{0,16},{8,24},{16,0},{24,8},{1,17},{9,25},{17,1},{25,9},{2,18},{10... | collective-permute-start | bytes 460808 | tf_op jit(solution)/shard_map/ppermute | solution.py:353
  337.1 5.3 %collective-permute-start.29 = (bf16[1,100,768]{2,1,0:T(8,128)(2,1)S(1)}, bf16[1,100,768]{2,1,0:T(8,128)(2,1)S(1)}, u32[]{:S(2)}, u32[]{:S(2)}) collective-permute-start(bf16[1,100,768]{2,1,0:T(8,128)(2,1)S(1)} %get-tuple-element.103), channel_id=1, source_target_pairs={{0,24},{8,0},{16,8},{24,16},{1,25},{9,1},{17,9},{25,17},{2,26},{10... | collective-permute-start | bytes 460808 | tf_op jit(solution)/shard_map/ppermute | solution.py:353
  342.8 3.6 copy-start.7
  (14 other events, 17.0 us)
Sparse Core Ops, SparseCore 0:
  9.9 59.7 all-gather.3
  71.6 57.0 all-gather.5
  173.0 55.9 reduce-scatter.2
  231.8 63.5 reduce-scatter.4
where the time goes:
time: 362 us; the launch traced here: 361 us
  waiting for transfers between devices  120 us (33%)
  starting transfers between devices  84.9 us (23%)
  Pallas kernels  54.1 us (15%)
  local copies, waits for them, and re-layouts  51.8 us (14%)
  other arithmetic  21.4 us (6%)
  between operations  14.6 us (4%)
  matrix products  11 us (3%)
    all_to_all x6, waiting for transfers between devices, exchange(): lax.all_to_all(parts, axis_name, split_axis=0, concat_axis=0, tiled=True)  54.9 us
    all_to_all x6, starting transfers between devices, exchange(): lax.all_to_all(parts, axis_name, split_axis=0, concat_axis=0, tiled=True)  34 us
    ppermute x14, waiting for transfers between devices, reduce_rows(): lax.ppermute(lax.dynamic_index_in_dim(parts, target, 0, False).astype(BF1...  29.6 us
    ppermute x10, waiting for transfers between devices, gather_rows(): lax.ppermute(rows, axis_name, [(j, (j + shift) % count) for j in range(co...  23.1 us
    pallas_call x1, Pallas kernels, expert_pass(): pl.pallas_call(partial(expert_kernel, experts), grid=(units // block,), i...  21.8 us
    ppermute x6, starting transfers between devices, exchange_by_permutes(): lax.ppermute(piece_for(lax.rem(place + shift, count)), axis_name, [(j, (j...  18.4 us
    pallas_call x1, Pallas kernels, attention_backward(): pl.pallas_call(partial(backward_kernel, heads, head_size, rows), grid=(le...  16.9 us
    ppermute x14, starting transfers between devices, reduce_rows(): lax.ppermute(lax.dynamic_index_in_dim(parts, target, 0, False).astype(BF1...  16.8 us
  transfers between devices with their start and end apart: 40, of which 17 were waited for; matrix products, arithmetic and copies ran while one was open for 19% of the time, Pallas kernels for 9%

commit v1 on v0

--- a/solution.py
+++ b/solution.py
@@ -126,7 +126,7 @@
 
 def backward_kernel(
     heads, head_size, row_count, qkv_ref, probs_ref, grad_ref, weight_ref, tokens_ref, normed_ref,
-    weight_grad_ref, token_grad_ref, gain_grad_ref, offset_ref,
+    context_ref, out_grad_ref, output_grad_ref, weight_grad_ref, token_grad_ref, gain_grad_ref, offset_ref,
     parts, dqueries, dkeys, dvalues, diagonals,
 ):
     block = pl.program_id(0)
@@ -140,6 +140,10 @@
             made = qkv_ref[kind]
             for head in range(heads):
                 parts[kind * heads + head] = made[:, head * head_size : (head + 1) * head_size]
+        output_grad = dot_tn(context_ref[...], out_grad_ref[...])
+        lanes = output_grad_ref.shape[2]
+        for part in range(output_grad_ref.shape[0]):
+            output_grad_ref[part] = output_grad[:, part * lanes : (part + 1) * lanes]
         dkeys[...] = jnp.zeros_like(dkeys)
         dvalues[...] = jnp.zeros_like(dvalues)
         diagonals[...] = jnp.zeros_like(diagonals)
@@ -191,7 +195,9 @@
             offset_ref[head : head + 1, :] = jnp.sum(part, axis=0, keepdims=True)
 
 
-def attention_backward(qkv, probs, grad, weight, tokens, normed, heads, head_size):
+def attention_backward(
+    qkv, probs, grad, weight, tokens, normed, context, out_grad, heads, head_size, parts
+):
     length, model_width = tokens.shape
     rows = 256
     width = heads * head_size
@@ -206,14 +212,18 @@
             pl.BlockSpec((3, model_width, width), lambda i: (0, 0, 0)),
             pl.BlockSpec((length, model_width), lambda i: (0, 0)),
             pl.BlockSpec((length, model_width), lambda i: (0, 0)),
+            pl.BlockSpec(context.shape, lambda i: (0, 0)),
+            pl.BlockSpec(context.shape, lambda i: (0, 0)),
         ],
         out_specs=[
+            pl.BlockSpec((parts, model_width, model_width // parts), lambda i: (0, 0, 0)),
             pl.BlockSpec((3, model_width, width), lambda i: (0, 0, 0)),
             pl.BlockSpec((length, model_width), lambda i: (0, 0)),
             pl.BlockSpec((1, model_width), lambda i: (0, 0)),
             pl.BlockSpec((padded_heads, 2 * length), lambda i: (0, 0)),
         ],
         out_shape=[
+            jax.ShapeDtypeStruct((parts, model_width, model_width // parts), F32),
             jax.ShapeDtypeStruct((3, model_width, width), F32),
             jax.ShapeDtypeStruct((length, model_width), BF16),
             jax.ShapeDtypeStruct((1, model_width), F32),
@@ -232,7 +242,7 @@
             bytes_accessed=16 * 1024 * 1024,
             transcendentals=0,
         ),
-    )(qkv, probs, grad, weight, tokens, normed)
+    )(qkv, probs, grad, weight, tokens, normed, context, out_grad)
 
 
 def expert_kernel(
@@ -386,11 +396,6 @@
     return [
         lax.select_n(lax.rem(place + count - origin, count), *held) for origin in range(count)
     ]
-
-
-def quarters(parts, count):
-    lead, rows, lanes = parts.shape
-    return parts.reshape(lead, count, rows // count, lanes).transpose(1, 0, 2, 3)
 
 
 def after(value, *earlier):
@@ -441,22 +446,41 @@
         [attention_gain, feedforward_gain, position_bias, router_matrix.reshape(-1)]
     )
     small_size = small.shape[0]
-    small_rows = -(-small_size // (16 * width)) * 16
+    step_rows = 16 * rep_count
+    part_rows = -(-(3 * shard_rows + -(-small_size // width)) // step_rows) * step_rows
+    small_rows = part_rows - 3 * shard_rows
     small = jnp.pad(small, (0, small_rows * width - small_size)).reshape(small_rows, width)
-    stacked = jnp.concatenate([query_weight, key_weight, value_weight], axis=0)
-
-    def weight_piece(target):
-        columns = lax.dynamic_slice_in_dim(stacked, target * width, width, 1)
-        return jnp.concatenate([columns, small], axis=0)
-
-    packed = jnp.stack(exchange_by_permutes(weight_piece, "seq"))
-    whole_tokens = gather_rows(after(token_rows, packed), "seq")
-    packed = lax.all_gather(packed, "shard", axis=1)
-    qkv_weight = packed[:, :, : 3 * shard_rows].reshape(
+    whole_tokens = gather_rows(token_rows, "seq")
+    quarter = model_width // rep_count
+    slice_rows = part_rows // rep_count
+    rep_place = lax.axis_index("rep")
+    stacked = jnp.concatenate(
+        [query_weight, key_weight, value_weight, jnp.tile(small, (1, seq_count))], axis=0
+    )
+    stacked = lax.dynamic_slice_in_dim(stacked, rep_place * slice_rows, slice_rows, 0)
+    output_columns = lax.dynamic_slice_in_dim(output_weight, rep_place * quarter, quarter, 1)
+    output_columns = output_columns.reshape(-1, width)
+
+    stacked = stacked.reshape(slice_rows, seq_count, width).transpose(1, 0, 2)
+    output_columns = jnp.broadcast_to(
+        output_columns[None], (seq_count,) + output_columns.shape
+    )
+    seq_packed = exchange(jnp.concatenate([stacked, output_columns], axis=1), "seq")
+    rep_packed = exchange(
+        jnp.broadcast_to(seq_packed[None], (rep_count,) + seq_packed.shape), "rep"
+    )
+    packed = jnp.stack(exchange_by_permutes(lambda target: rep_packed, "shard"))
+    parts = packed[:, :, :, :slice_rows].transpose(2, 0, 1, 3, 4)
+    parts = parts.reshape(seq_count, shard_count, part_rows, width)
+    qkv_weight = parts[:, :, : 3 * shard_rows].reshape(
         seq_count, shard_count, 3, shard_rows, width
     )
     qkv_weight = qkv_weight.transpose(2, 0, 1, 3, 4).reshape(3, model_width, width)
-    small_all = packed[:, :, 3 * shard_rows :].reshape(owner_count, -1)
+    small_all = parts[:, :, 3 * shard_rows :].reshape(owner_count, -1)
+    output_all = packed[:, :, :, slice_rows:].reshape(
+        shard_count, rep_count, seq_count, shard_rows, quarter
+    )
+    output_all = output_all.transpose(2, 0, 3, 1, 4).reshape(model_width, model_width)
     at = 0
     pieces = []
     for size in (shard_rows, shard_rows, position_bias.shape[0], router_matrix.size):
@@ -478,8 +502,10 @@
         slot_index[None, :] == jnp.arange(slots, dtype=jnp.int32)[:, None]
     ).astype(BF16)
 
-    def dispatch(rows):
-        placed = dot_nn(place_marks, rows).astype(BF16)
+    def place_rows(rows):
+        return dot_nn(place_marks, rows).astype(BF16)
+
+    def dispatch(placed):
         arrived = exchange(placed.reshape(experts, capacity, model_width), group)
         return arrived.reshape(slots, model_width)
 
@@ -487,8 +513,6 @@
         back = exchange(rows.reshape(experts, capacity, model_width), group)
         return back.reshape(slots, model_width)
 
-    output_seq = gather_rows(after(output_weight, whole_tokens), "seq")
-    expert_grads = dispatch(after(grad_rows, whole_tokens, qkv_weight))
     up_full = lax.all_gather(up_weight, "rep", axis=1, tiled=True)[0]
     down_full = lax.all_gather(down_weight, "rep", axis=1, tiled=True)[0]
 
@@ -501,14 +525,15 @@
     own_table = jnp.pad(own_table, ((0, 0), (0, padded_heads - heads)))
     skewed = skew_bias(dot_tn(own_table, bucket_marks), heads)
 
+    placed_grads = place_rows(grad_rows)
+    whole_tokens, skewed, qkv_weight, placed_grads = lax.optimization_barrier(
+        (whole_tokens, skewed, qkv_weight, placed_grads)
+    )
+    expert_grads = dispatch(placed_grads)
+
     normed_whole, qkv, probs, context_own = attention_forward(
         whole_tokens, gain_a, qkv_weight, skewed, heads, head_size
     )
-    output_seq = after(output_seq, context_own)
-    output_all = gather_rows(output_seq, "shard").reshape(
-        shard_count, seq_count, shard_rows, model_width
-    )
-    output_all = output_all.transpose(1, 0, 2, 3).reshape(model_width, model_width)
     context_own = after(context_own, expert_grads)
     context = exchange(context_own.reshape(seq_count, seg_rows, width), "seq")
     context = context.transpose(1, 0, 2).reshape(seg_rows, model_width)
@@ -518,7 +543,7 @@
     middle_inverse = inverse_rms(middle)
     normed_ffn = (middle * middle_inverse * gain_f).astype(BF16)
 
-    expert_rows = dispatch(normed_ffn)
+    expert_rows = dispatch(place_rows(normed_ffn))
     owner = seq_place * shard_count + lax.axis_index("shard")
     lanes = -(-experts // TILE) * TILE
     router_lanes = jnp.pad(full_router, ((0, 0), (0, lanes - experts)))
@@ -542,17 +567,17 @@
     context_grad = dot_nt(attn_out_grad, output_all).astype(BF16)
     context_grad = context_grad.reshape(seg_rows, seq_count, width).transpose(1, 0, 2)
     context_grad = exchange(context_grad, "seq").reshape(length, width)
-    output_grad = dot_tn(context, attn_out_grad).reshape(
-        seq_count, shard_count, shard_rows, model_width
-    )
-    output_grad = reduce_rows(output_grad.transpose(1, 0, 2, 3), "shard")
-    output_grad = reduce_rows(quarters(output_grad, rep_count), "rep")
     returned = send_back(after(gated_out, context_grad))
 
-    qkv_grad, normed_grad_part, gain_a_grad, offset_grad = attention_backward(
-        qkv, probs, context_grad, qkv_weight, whole_tokens, normed_whole, heads, head_size
-    )
-    output_part = reduce_rows(output_grad, "seq")
+    output_grad, qkv_grad, normed_grad_part, gain_a_grad, offset_grad = attention_backward(
+        qkv, probs, context_grad, qkv_weight, whole_tokens, normed_whole,
+        context, attn_out_grad, heads, head_size, rep_count,
+    )
+    output_grad = output_grad.reshape(rep_count, seq_count, shard_count, shard_rows, quarter)
+    output_grad = output_grad.transpose(2, 0, 1, 3, 4)
+    output_grad = output_grad.reshape(shard_count, rep_count, seq_count, -1, width)
+    normed_grad_part = after(normed_grad_part, returned)
+    qkv_grad = after(qkv_grad, returned)
     layer_output = (middle + dot_tn(place_marks, returned)).astype(BF16)
     own_table_grad = lax.dot_general(
         bucket_marks.astype(F32),
@@ -565,6 +590,10 @@
         jnp.zeros((BUCKETS, head_count), F32), own_table_grad[:, :heads], seq_place * heads, 1
     )
 
+    normed_grad = reduce_rows(
+        normed_grad_part.reshape(seq_count, seg_rows, model_width), "seq"
+    )
+
     small_grad = jnp.concatenate(
         [
             gain_a_grad.reshape(owner_count, -1),
@@ -581,25 +610,39 @@
     )
     small_grad = small_grad.reshape(seq_count, shard_count, small_rows, width)
     weight_parts = jnp.concatenate([weight_parts, small_grad.transpose(1, 0, 2, 3)], axis=2)
-    weight_parts = reduce_rows(weight_parts, "shard")
-    weight_parts = reduce_rows(quarters(weight_parts, rep_count), "rep").astype(BF16)
+    weight_parts = weight_parts.reshape(shard_count, seq_count, rep_count, slice_rows, width)
+    weight_parts = jnp.concatenate([weight_parts.transpose(0, 2, 1, 3, 4), output_grad], axis=3)
+    weight_parts = reduce_rows(reduce_rows(weight_parts, "shard"), "rep").astype(BF16)
+    weight_parts, normed_grad, up_weight_grad = lax.optimization_barrier(
+        (weight_parts, normed_grad, up_weight_grad)
+    )
     weight_parts = exchange_by_permutes(
         lambda target: lax.dynamic_index_in_dim(weight_parts, target, 0, False), "seq"
     )
-    weight_rows = jnp.concatenate(weight_parts, axis=1)
-    normed_grad = reduce_rows(
-        normed_grad_part.reshape(seq_count, seg_rows, model_width), "seq"
-    )
     token_inverse = inverse_rms(inputs)
     token_input_gradient = middle_grad + norm_backward(inputs, token_inverse, gain_a, normed_grad)
 
-    rows = jnp.concatenate([weight_rows, output_part.astype(BF16)], axis=0)
-    rows = gather_rows(rows[None], "rep").astype(F32)
-    part_rows = weight_rows.shape[0]
-    weight_rows = rows[:, :part_rows].reshape(rep_count * part_rows, model_width)
-    output_rows = rows[:, part_rows:].reshape(shard_rows, model_width)
+    output_part = sum(part[slice_rows:].astype(F32) for part in weight_parts).astype(BF16)
+    slices = jnp.concatenate([part[:slice_rows] for part in weight_parts] + [output_part], axis=0)
+    slices = exchange_by_permutes(lambda target: slices, "rep")
+    weight_rows = jnp.concatenate(
+        [
+            jnp.concatenate(
+                [
+                    part[origin * slice_rows : (origin + 1) * slice_rows]
+                    for origin in range(seq_count)
+                ],
+                axis=1,
+            )
+            for part in slices
+        ],
+        axis=0,
+    ).astype(F32)
     matrices = [weight_rows[k * shard_rows : (k + 1) * shard_rows] for k in range(3)]
-    matrices.append(output_rows)
+    output_slices = [
+        part[seq_count * slice_rows :].reshape(shard_rows, quarter) for part in slices
+    ]
+    matrices.append(jnp.concatenate(output_slices, axis=1).astype(F32))
     smalls = weight_rows[3 * shard_rows :].reshape(small_rows, seq_count, width)
     smalls = jnp.sum(smalls, axis=1).reshape(-1)[:small_size]
     table_size = position_bias.shape[0]

time: 362 us -> 327 us (0.903)
  starting transfers between devices: 84.9 us -> 60.4 us
  blocking collectives: 2.68 us -> 23.4 us
  waiting for transfers between devices: 120 us -> 104 us
  local copies, waits for them, and re-layouts: 51.8 us -> 38.5 us
    all_to_all x0 -> x1, blocking collectives: none -> 23.4 us  [exchange(): lax.all_to_all(parts, axis_name, split_axis=0, concat_axis=0, tiled=True)]
    ppermute x10 -> x3, waiting for transfers between devices: 23.1 us -> 6.8 us  [gather_rows(): lax.ppermute(rows, axis_name, [(j, (j + shift) % count) for j in range(co...]
    ppermute x10 -> x3, starting transfers between devices: 15.5 us -> 3.82 us  [gather_rows(): lax.ppermute(rows, axis_name, [(j, (j + shift) % count) for j in range(co...]
    all_to_all x6 -> x7, waiting for transfers between devices: 54.9 us -> 64.1 us  [exchange(): lax.all_to_all(parts, axis_name, split_axis=0, concat_axis=0, tiled=True)]
    ppermute x6 -> x7, starting transfers between devices: 18.4 us -> 9.88 us  [exchange_by_permutes(): lax.ppermute(piece_for(lax.rem(place + shift, count)), axis_name, [(j, (j...]
    ppermute x14 -> x7, waiting for transfers between devices: 29.6 us -> 22.7 us  [reduce_rows(): lax.ppermute(lax.dynamic_index_in_dim(parts, target, 0, False).astype(BF1...]
    ppermute x14 -> x7, starting transfers between devices: 16.8 us -> 11.4 us  [reduce_rows(): lax.ppermute(lax.dynamic_index_in_dim(parts, target, 0, False).astype(BF1...]
    convert_element_type x5 -> x1, local copies, waits for them, and re-layouts: 4.64 us -> 0.12 us  [reduce_rows(): lax.dynamic_index_in_dim(parts, target, 0, False).astype(BF16)]
  transfers between devices with their start and end apart: 40 -> 28, of which waited for: 17 -> 15; matrix products, arithmetic and copies ran while one was open for 19% -> 14% of each run, Pallas kernels for 9% -> 10%
where the time goes in v1:
time: 327 us; the launch traced here: 326 us
  waiting for transfers between devices  104 us (32%)
  starting transfers between devices  60.4 us (18%)
  Pallas kernels  55.2 us (17%)
  local copies, waits for them, and re-layouts  38.5 us (12%)
  blocking collectives  23.4 us (7%)
  other arithmetic  20.8 us (6%)
  between operations  14.5 us (4%)
  matrix products  9.5 us (3%)
    all_to_all x7, waiting for transfers between devices, exchange(): lax.all_to_all(parts, axis_name, split_axis=0, concat_axis=0, tiled=True)  64.1 us
    all_to_all x7, starting transfers between devices, exchange(): lax.all_to_all(parts, axis_name, split_axis=0, concat_axis=0, tiled=True)  35.2 us
    all_to_all x1, blocking collectives, exchange(): lax.all_to_all(parts, axis_name, split_axis=0, concat_axis=0, tiled=True)  23.4 us
    ppermute x7, waiting for transfers between devices, reduce_rows(): lax.ppermute(lax.dynamic_index_in_dim(parts, target, 0, False).astype(BF1...  22.7 us
    pallas_call x1, Pallas kernels, expert_pass(): pl.pallas_call(partial(expert_kernel, experts), grid=(units // block,), i...  21.3 us
    pallas_call x1, Pallas kernels, attention_backward(): pl.pallas_call(partial(backward_kernel, heads, head_size, rows), grid=(le...  18.6 us
    unnamed x78, local copies, waits for them, and re-layouts  17.7 us
    pallas_call x1, Pallas kernels, attention_forward(): pl.pallas_call(partial(forward_kernel, heads, head_size, rows), grid=(len...  13.4 us
  transfers between devices with their start and end apart: 28, of which 15 were waited for; matrix products, arithmetic and copies ran while one was open for 14% of the time, Pallas kernels for 10%

profile of v1, /device:TPU:0, one launch (start us, length us, event | category | flops | bytes accessed | tf_op | source)
XLA Modules:
  0.0 325.9 jit_solution(15823989414142394804)
XLA Ops:
  11.2 6.3 %all-to-all-start = ((bf16[4,176,192]{2,1,0:T(8,128)(2,1)}), bf16[4,176,192]{2,1,0:T(8,128)(2,1)S(1)}, u32[]{:S(2)}, u32[]{:S(2)}) async-start(bf16[4,176,192]{2,1,0:T(8,128)(2,1)} %pad_maximum_fusion.2), calls=%async_computation | async-start | bytes 720896 | tf_op jit(solution)/shard_map/all_to_all | solution.py:406
  18.3 10.2 %all-to-all-done = bf16[4,176,192]{2,1,0:T(8,128)(2,1)S(1)} async-done(((bf16[4,176,192]{2,1,0:T(8,128)(2,1)}), bf16[4,176,192]{2,1,0:T(8,128)(2,1)S(1)}, u32[]{:S(2)}, u32[]{:S(2)}) %all-to-all-start) | async-done | bytes 270368 | tf_op jit(solution)/shard_map/all_to_all | solution.py:406
  28.5 1.2 broadcast_in_dim.18
  29.7 3.9 %all-to-all-start.1 = ((bf16[4,4,176,192]{3,2,1,0:T(8,128)(2,1)}), bf16[4,4,176,192]{3,2,1,0:T(8,128)(2,1)S(1)}, u32[]{:S(2)}, u32[]{:S(2)}) async-start(bf16[4,4,176,192]{3,2,1,0:T(8,128)(2,1)} %broadcast_in_dim.18), calls=%async_computation.1 | async-start | bytes 2883584 | tf_op jit(solution)/shard_map/all_to_all | solution.py:406
  33.6 2.0 collective-permute-start.1
  35.6 1.8 collective-permute-start.2
  38.4 13.5 %all-to-all-done.1 = bf16[4,4,176,192]{3,2,1,0:T(8,128)(2,1)S(1)} async-done(((bf16[4,4,176,192]{3,2,1,0:T(8,128)(2,1)}), bf16[4,4,176,192]{3,2,1,0:T(8,128)(2,1)S(1)}, u32[]{:S(2)}, u32[]{:S(2)}) %all-to-all-start.1) | async-done | bytes 1081376 | tf_op jit(solution)/shard_map/all_to_all | solution.py:406
  51.9 1.3 convolution_convert_fusion.1
  53.3 1.1 constant_dynamic-update-slice_fusion.2
  54.4 6.8 %collective-permute-done.1 = bf16[256,768]{1,0:T(8,128)(2,1)S(1)} collective-permute-done((bf16[256,768]{1,0:T(8,128)(2,1)S(1)}, bf16[256,768]{1,0:T(8,128)(2,1)S(1)}, u32[]{:S(2)}, u32[]{:S(2)}) %collective-permute-start.1) | collective-permute-done | bytes 393248 | tf_op jit(solution)/shard_map/ppermute | solution.py:363
  61.3 1.1 copy-done.22
  62.5 1.6 select_bitcast_fusion.1
  66.4 2.0 shard_map.229.skewed_ref
  68.4 1.7 copy-done.2
  70.2 9.3 %all-to-all-start.2 = ((bf16[8,64,768]{2,1,0:T(8,128)(2,1)}), bf16[8,64,768]{2,1,0:T(8,128)(2,1)S(1)}, u32[]{:S(2)}, u32[]{:S(2)}) async-start(bf16[8,64,768]{2,1,0:T(8,128)(2,1)} %bitcast.161), calls=%async_computation.2 | async-start | bytes 1572864 | tf_op jit(solution)/shard_map/all_to_all | solution.py:406
  79.6 13.4 %shard_map.230 = (bf16[1024,768]{1,0:T(8,128)(2,1)S(1)}, bf16[3,1024,192]{2,1,0:T(8,128)(2,1)S(1)}, bf16[3,1024,1024]{2,1,0:T(8,128)(2,1)}, bf16[1024,192]{1,0:T(8,128)(2,1)S(1)}) custom-call(bf16[1024,768]{1,0:T(8,128)(2,1)} %copy-done.22, f32[1,768]{1,0:T(1,128)S(1)} %reshape.264.gain_ref, bf16[3,768,192]{2,1,0:T(8,128)(2,1)S(1)} %bitcast.133, ...), custom_call_target="tpu_custom_call" | custom-call | flops 1711276032 | bytes 16777216 | tf_op jit(solution)/shard_map/pallas_call | solution.py:96
  93.0 1.2 copy-done.3
  94.2 1.1 copy-done.4
  95.3 5.1 %all-to-all-done.2 = bf16[8,64,768]{2,1,0:T(8,128)(2,1)S(1)} async-done(((bf16[8,64,768]{2,1,0:T(8,128)(2,1)}), bf16[8,64,768]{2,1,0:T(8,128)(2,1)S(1)}, u32[]{:S(2)}, u32[]{:S(2)}) %all-to-all-start.2) | async-done | bytes 786464 | tf_op jit(solution)/shard_map/all_to_all | solution.py:406
  100.4 1.0 copy.48
  101.4 3.6 %all-to-all-start.3 = ((bf16[4,256,192]{1,2,0:T(8,128)(2,1)}), bf16[4,256,192]{1,2,0:T(8,128)(2,1)S(1)}, u32[]{:S(2)}, u32[]{:S(2)}) async-start(bf16[4,256,192]{1,2,0:T(8,128)(2,1)} %copy.48), calls=%async_computation.3 | async-start | bytes 786432 | tf_op jit(solution)/shard_map/all_to_all | solution.py:406
  105.0 1.7 fusion.5
  106.7 2.4 copy.49
  109.1 4.1 %reshape.243 = bf16[768,768]{1,0:T(8,128)(2,1)} reshape(bf16[4,2,96,4,192]{4,3,2,1,0:T(4,128)(2,1)} %copy.49) | data formatting | bytes 2359296 | tf_op jit(solution)/shard_map/reshape | solution.py:483
  113.3 3.3 %all-to-all-done.3 = bf16[4,256,192]{1,2,0:T(8,128)(2,1)S(1)} async-done(((bf16[4,256,192]{1,2,0:T(8,128)(2,1)}), bf16[4,256,192]{1,2,0:T(8,128)(2,1)S(1)}, u32[]{:S(2)}, u32[]{:S(2)}) %all-to-all-start.3) | async-done | bytes 393248 | tf_op jit(solution)/shard_map/all_to_all | solution.py:406
  117.3 2.0 multiply_reduce_fusion.2
  119.3 1.3 convolution_convert_fusion
  120.7 3.5 %all-to-all-start.4 = ((bf16[8,64,768]{2,1,0:T(8,128)(2,1)}), bf16[8,64,768]{2,1,0:T(8,128)(2,1)S(1)}, u32[]{:S(2)}, u32[]{:S(2)}) async-start(bf16[8,64,768]{2,1,0:T(8,128)(2,1)} %bitcast.160), calls=%async_computation.4 | async-start | bytes 1572864 | tf_op jit(solution)/shard_map/all_to_all | solution.py:406
  124.7 20.4 %all-to-all-done.4 = bf16[8,64,768]{2,1,0:T(8,128)(2,1)S(1)} async-done(((bf16[8,64,768]{2,1,0:T(8,128)(2,1)}), bf16[8,64,768]{2,1,0:T(8,128)(2,1)S(1)}, u32[]{:S(2)}, u32[]{:S(2)}) %all-to-all-start.4) | async-done | bytes 786464 | tf_op jit(solution)/shard_map/all_to_all | solution.py:406
  145.1 21.3 %shard_map.231 = (bf16[3072,768]{1,0:T(8,128)(2,1)}, bf16[3072,768]{1,0:T(8,128)(2,1)}, bf16[512,768]{1,0:T(8,128)(2,1)S(1)}, bf16[512,768]{1,0:T(8,128)(2,1)S(1)}, bf16[512,128]{1,0:T(8,128)(2,1)S(1)}) custom-call(bf16[512,768]{1,0:T(8,128)(2,1)S(1)} %bitcast.135, bf16[512,768]{1,0:T(8,128)(2,1)S(1)} %bitcast.141, bf16[768,128]{1,0:T(8,128)(2,1)S(1)} %pad.23.router_ref, ...), custom_call_target="tpu_custom_call" | custom-call | flops 14495514624 | bytes 16777216 | tf_op jit(solution)/shard_map/pallas_call | solution.py:305
  169.4 23.4 %all_to_all.40 = bf16[8,64,768]{2,1,0:T(8,128)(2,1)S(1)} all-to-all(bf16[8,64,768]{2,1,0:T(8,128)(2,1)S(1)} %bitcast.142), channel_id=1, replica_groups=mesh['rep'=4,'seq'=4,'shard'=2] {'seq','shard'}, dimensions={0} | all-to-all | bytes 1572864 | tf_op jit(solution)/shard_map/all_to_all | solution.py:406
  196.4 4.1 %all-to-all-start.6 = ((bf16[4,256,192]{1,2,0:T(8,128)(2,1)}), bf16[4,256,192]{1,2,0:T(8,128)(2,1)}, u32[]{:S(2)}, u32[]{:S(2)}) async-start(bf16[4,256,192]{1,2,0:T(8,128)(2,1)} %bitcast.27), calls=%async_computation.6 | async-start | bytes 786432 | tf_op jit(solution)/shard_map/all_to_all | solution.py:406
  200.7 11.5 %all-to-all-done.6 = bf16[4,256,192]{1,2,0:T(8,128)(2,1)} async-done(((bf16[4,256,192]{1,2,0:T(8,128)(2,1)}), bf16[4,256,192]{1,2,0:T(8,128)(2,1)}, u32[]{:S(2)}, u32[]{:S(2)}) %all-to-all-start.6) | async-done | bytes 393248 | tf_op jit(solution)/shard_map/all_to_all | solution.py:406
  212.2 1.2 copy.51
  213.4 4.4 %all-to-all-start.7 = ((bf16[8,64,768]{2,1,0:T(8,128)(2,1)}), bf16[8,64,768]{2,1,0:T(8,128)(2,1)}, u32[]{:S(2)}, u32[]{:S(2)}) async-start(bf16[8,64,768]{2,1,0:T(8,128)(2,1)} %bitcast.140), calls=%async_computation.7 | async-start | bytes 1572864 | tf_op jit(solution)/shard_map/all_to_all | solution.py:406
  217.8 1.2 fusion.32
  219.0 1.2 reshape.257
  220.3 1.5 copy-done.5
  221.7 18.6 %shard_map.232 = (f32[4,768,192]{2,1,0:T(8,128)}, f32[3,768,192]{2,1,0:T(8,128)}, bf16[1024,768]{1,0:T(8,128)(2,1)S(1)}, f32[1,768]{1,0:T(1,128)S(1)}, f32[8,2048]{1,0:T(8,128)S(1)}) custom-call(bf16[3,1024,192]{2,1,0:T(8,128)(2,1)S(1)} %copy-done.5, bf16[3,1024,1024]{2,1,0:T(8,128)(2,1)} %get-tuple-element.47.probs_ref, bf16[1024,192]{1,0:T(8,128)(2,1)S(1)} %bitcast.137, ...), custom_call_target="tpu_custom_call" | custom-call | flops 3422552064 | bytes 16777216 | tf_op jit(solution)/shard_map/pallas_call | solution.py:205
  240.3 1.1 copy-done.6
  242.4 1.8 copy.53
  244.4 2.6 copy-done.18
  247.1 1.2 fusion.6
  249.1 3.8 %collective-permute-start.10 = (bf16[256,768]{1,0:T(8,128)(2,1)S(1)}, bf16[256,768]{1,0:T(8,128)(2,1)S(1)}, u32[]{:S(2)}, u32[]{:S(2)}) collective-permute-start(bf16[256,768]{1,0:T(8,128)(2,1)S(1)} %get-tuple-element.96), channel_id=1, source_target_pairs={{0,6},{2,0},{4,2},{6,4},{1,7},{3,1},{5,3},{7,5},{8,14},{10,8},{12,... | collective-permute-start | bytes 1179656 | tf_op jit(solution)/shard_map/ppermute | solution.py:375
  253.0 1.2 collective-permute-start.9
  254.1 2.3 fusion.8
  256.4 2.2 fusion.4
  258.8 1.9 collective-permute-start.5
  260.7 1.2 collective-permute-start.6
  262.4 2.6 collective-permute-start.7
  265.0 6.9 %collective-permute-done.8 = bf16[256,768]{1,0:T(8,128)(2,1)S(1)} collective-permute-done((bf16[256,768]{1,0:T(8,128)(2,1)S(1)}, bf16[256,768]{1,0:T(8,128)(2,1)S(1)}, u32[]{:S(2)}, u32[]{:S(2)}) %collective-permute-start.8) | collective-permute-done | bytes 393248 | tf_op jit(solution)/shard_map/ppermute | solution.py:375
  272.0 15.2 %collective-permute-done.9 = bf16[256,768]{1,0:T(8,128)(2,1)S(1)} collective-permute-done((bf16[256,768]{1,0:T(8,128)(2,1)S(1)}, bf16[256,768]{1,0:T(8,128)(2,1)S(1)}, u32[]{:S(2)}, u32[]{:S(2)}) %collective-permute-start.9) | collective-permute-done | bytes 393248 | tf_op jit(solution)/shard_map/ppermute | solution.py:375
  288.3 2.9 convert_element_type.195
  291.3 3.9 %collective-permute-start.11 = (bf16[176,192]{1,0:T(8,128)(2,1)S(1)}, bf16[176,192]{1,0:T(8,128)(2,1)S(1)}, u32[]{:S(2)}, u32[]{:S(2)}) collective-permute-start(bf16[176,192]{1,0:T(8,128)(2,1)S(1)} %get-tuple-element.111), channel_id=1, source_target_pairs={{0,2},{2,4},{4,6},{6,0},{1,3},{3,5},{5,7},{7,1},{8,10},{10,12},{12... | collective-permute-start | bytes 202760 | tf_op jit(solution)/shard_map/ppermute | solution.py:390
  295.2 2.4 collective-permute-start.13
  298.7 3.1 collective-permute-done.12
  302.6 1.7 collective-permute-start.15
  304.3 1.3 collective-permute-start.16
  305.5 1.2 fusion.13
  306.8 2.8 convert_element_type.205
  310.4 1.4 collective-permute-done.15
  311.7 2.0 collective-permute-done.16
  313.7 1.2 select_select_fusion.3
  315.3 0.9 fusion.60
  (186 shorter events, 26.0 us)
Async XLA Ops:
  7.2 3.2 copy-start
  7.2 2.7 copy-start.31
  7.2 2.7 copy-start.32
  7.2 2.7 copy-start.33
  7.2 137.9 %all-gather.3.cloned.1.call-start = ((), (), s32[]{:S(2)}) async-start(), calls=%async_computation.10 | async-start | bytes 5898240 | tf_op jit(solution)/shard_map/all_gather | solution.py:516
  11.2 17.3 %all-to-all-start = ((bf16[4,176,192]{2,1,0:T(8,128)(2,1)}), bf16[4,176,192]{2,1,0:T(8,128)(2,1)S(1)}, u32[]{:S(2)}, u32[]{:S(2)}) async-start(bf16[4,176,192]{2,1,0:T(8,128)(2,1)} %pad_maximum_fusion.2), calls=%async_computation | async-start | bytes 720896 | tf_op jit(solution)/shard_map/all_to_all | solution.py:406
  17.6 127.6 %all-gather.5.cloned.1.call-start = ((), (), s32[]{:S(2)}) async-start(), calls=%async_computation.11 | async-start | bytes 5898240 | tf_op jit(solution)/shard_map/all_gather | solution.py:517
  29.7 3.9 %copy-start.23 = (bf16[1,256,768]{2,1,0:T(8,128)(2,1)S(1)}, bf16[1,256,768]{2,1,0:T(8,128)(2,1)}, u32[]{:S(2)}) copy-start(bf16[1,256,768]{2,1,0:T(8,128)(2,1)} %param.14) | copy-start | bytes 1179652
  29.7 7.7 %copy-start.34 = (s32[1,256,1]{1,2,0:T(1,128)S(1)}, s32[1,256,1]{1,2,0:T(1,128)}, u32[]{:S(2)}) copy-start(s32[1,256,1]{1,2,0:T(1,128)} %param.25) | copy-start | bytes 3076
  29.7 22.2 %copy-start.27 = (bf16[1,256,768]{2,1,0:T(8,128)(2,1)S(1)}, bf16[1,256,768]{2,1,0:T(8,128)(2,1)}, u32[]{:S(2)}) copy-start(bf16[1,256,768]{2,1,0:T(8,128)(2,1)} %param.15) | copy-start | bytes 1179652
  29.7 23.4 %copy-start.35 = (s32[2047]{0:T(1024)S(1)}, s32[2047]{0:T(1024)}, u32[]{:S(2)}) copy-start(s32[2047]{0:T(1024)} %param.22) | copy-start | bytes 24568
  29.7 22.1 %all-to-all-start.1 = ((bf16[4,4,176,192]{3,2,1,0:T(8,128)(2,1)}), bf16[4,4,176,192]{3,2,1,0:T(8,128)(2,1)S(1)}, u32[]{:S(2)}, u32[]{:S(2)}) async-start(bf16[4,4,176,192]{3,2,1,0:T(8,128)(2,1)} %broadcast_in_dim.18), calls=%async_computation.1 | async-start | bytes 2883584 | tf_op jit(solution)/shard_map/all_to_all | solution.py:406
  33.6 19.7 %collective-permute-start = (bf16[256,768]{1,0:T(8,128)(2,1)S(1)}, bf16[256,768]{1,0:T(8,128)(2,1)}, u32[]{:S(2)}, u32[]{:S(2)}) collective-permute-start(bf16[256,768]{1,0:T(8,128)(2,1)S(1)} %bitcast.149), channel_id=1, source_target_pairs={{0,2},{2,4},{4,6},{6,0},{1,3},{3,5},{5,7},{7,1},{8,10},{10,12},{12... | collective-permute-start | bytes 1179656 | tf_op jit(solution)/shard_map/ppermute | solution.py:363
  33.6 27.6 %collective-permute-start.1 = (bf16[256,768]{1,0:T(8,128)(2,1)S(1)}, bf16[256,768]{1,0:T(8,128)(2,1)S(1)}, u32[]{:S(2)}, u32[]{:S(2)}) collective-permute-start(bf16[256,768]{1,0:T(8,128)(2,1)S(1)} %bitcast.150), channel_id=1, source_target_pairs={{0,4},{2,6},{4,0},{6,2},{1,5},{3,7},{5,1},{7,3},{8,12},{10,14},{12... | collective-permute-start | bytes 1179656 | tf_op jit(solution)/shard_map/ppermute | solution.py:363
  35.6 25.6 %collective-permute-start.2 = (bf16[256,768]{1,0:T(8,128)(2,1)S(1)}, bf16[256,768]{1,0:T(8,128)(2,1)S(1)}, u32[]{:S(2)}, u32[]{:S(2)}) collective-permute-start(bf16[256,768]{1,0:T(8,128)(2,1)S(1)} %bitcast.151), channel_id=1, source_target_pairs={{0,6},{2,0},{4,2},{6,4},{1,7},{3,1},{5,3},{7,5},{8,14},{10,8},{12,... | collective-permute-start | bytes 1179656 | tf_op jit(solution)/shard_map/ppermute | solution.py:363
  51.9 10.6 %collective-permute-start.3 = (bf16[4,4,176,192]{3,2,1,0:T(8,128)(2,1)S(1)}, bf16[4,4,176,192]{3,2,1,0:T(8,128)(2,1)}, u32[]{:S(2)}, u32[]{:S(2)}) collective-permute-start(bf16[4,4,176,192]{3,2,1,0:T(8,128)(2,1)S(1)} %all-to-all-done.1), channel_id=1, source_target_pairs={{0,1},{1,0},{2,3},{3,2},{4,5},{5,4},{6,7},{7,6},{8,9},{9,8},{10,11... | collective-permute-start | bytes 3244040 | tf_op jit(solution)/shard_map/ppermute | solution.py:390
  61.3 1.1 copy-start.22
  64.0 1.1 copy-start.16
  64.0 1.6 copy-start.17
  68.4 1.7 copy-start.2
  70.2 30.3 %all-to-all-start.2 = ((bf16[8,64,768]{2,1,0:T(8,128)(2,1)}), bf16[8,64,768]{2,1,0:T(8,128)(2,1)S(1)}, u32[]{:S(2)}, u32[]{:S(2)}) async-start(bf16[8,64,768]{2,1,0:T(8,128)(2,1)} %bitcast.161), calls=%async_computation.2 | async-start | bytes 1572864 | tf_op jit(solution)/shard_map/all_to_all | solution.py:406
  93.0 1.2 copy-start.3
  94.2 1.1 copy-start.4
  101.4 15.2 %all-to-all-start.3 = ((bf16[4,256,192]{1,2,0:T(8,128)(2,1)}), bf16[4,256,192]{1,2,0:T(8,128)(2,1)S(1)}, u32[]{:S(2)}, u32[]{:S(2)}) async-start(bf16[4,256,192]{1,2,0:T(8,128)(2,1)} %copy.48), calls=%async_computation.3 | async-start | bytes 786432 | tf_op jit(solution)/shard_map/all_to_all | solution.py:406
  116.6 0.7 copy-start.25
  119.3 1.4 copy-start.11
  120.7 24.5 %all-to-all-start.4 = ((bf16[8,64,768]{2,1,0:T(8,128)(2,1)}), bf16[8,64,768]{2,1,0:T(8,128)(2,1)S(1)}, u32[]{:S(2)}, u32[]{:S(2)}) async-start(bf16[8,64,768]{2,1,0:T(8,128)(2,1)} %bitcast.160), calls=%async_computation.4 | async-start | bytes 1572864 | tf_op jit(solution)/shard_map/all_to_all | solution.py:406
  124.2 164.1 %reduce-scatter.3.cloned.1.call-start = ((), (), s32[]{:S(2)}) async-start(), calls=%async_computation.12 | async-start | bytes 5898240 | tf_op jit(solution)/shard_map/reduce_scatter | solution.py:557
  166.4 0.9 copy-start.8
  167.3 0.9 copy-start.9
  168.2 138.6 %reduce-scatter.5.cloned.1.call-start = ((), (), s32[]{:S(2)}) async-start(), calls=%async_computation.13 | async-start | bytes 5898240 | tf_op jit(solution)/shard_map/reduce_scatter | solution.py:560
  168.2 1.1 copy-start.10
  168.8 24.0 %copy-start.12 = (f32[256,768]{1,0:T(8,128)S(1)}, f32[256,768]{1,0:T(8,128)}, u32[]{:S(2)}) copy-start(f32[256,768]{1,0:T(8,128)} %copy-done.11) | copy-start | bytes 2359300
  192.8 1.0 copy-start.28
  193.3 0.9 copy-start.20
  193.3 1.6 copy-start.19
  194.9 5.6 %copy-start.26 = (bf16[4,256,192]{1,2,0:T(8,128)(2,1)S(1)}, bf16[4,256,192]{1,2,0:T(8,128)(2,1)}, u32[]{:S(2)}) copy-start(bf16[4,256,192]{1,2,0:T(8,128)(2,1)} %copy-done.25) | copy-start | bytes 1179652
  196.4 15.8 %all-to-all-start.6 = ((bf16[4,256,192]{1,2,0:T(8,128)(2,1)}), bf16[4,256,192]{1,2,0:T(8,128)(2,1)}, u32[]{:S(2)}, u32[]{:S(2)}) async-start(bf16[4,256,192]{1,2,0:T(8,128)(2,1)} %bitcast.27), calls=%async_computation.6 | async-start | bytes 786432 | tf_op jit(solution)/shard_map/all_to_all | solution.py:406
  213.4 29.0 %all-to-all-start.7 = ((bf16[8,64,768]{2,1,0:T(8,128)(2,1)}), bf16[8,64,768]{2,1,0:T(8,128)(2,1)}, u32[]{:S(2)}, u32[]{:S(2)}) async-start(bf16[8,64,768]{2,1,0:T(8,128)(2,1)} %bitcast.140), calls=%async_computation.7 | async-start | bytes 1572864 | tf_op jit(solution)/shard_map/all_to_all | solution.py:406
  220.3 1.5 copy-start.5
  240.3 1.1 copy-start.6
  244.2 2.8 copy-start.18
  244.4 3.9 %copy-start.14 = (f32[2,4,320,192]{3,2,1,0:T(8,128)}, f32[2,4,320,192]{3,2,1,0:T(8,128)S(1)}, u32[]{:S(2)}) copy-start(f32[2,4,320,192]{3,2,1,0:T(8,128)S(1)} %pad_maximum_fusion) | copy-start | bytes 5898244
  247.1 2.0 copy-start.7
  248.3 5.8 %copy-start.13 = (f32[256,768]{1,0:T(8,128)S(1)}, f32[256,768]{1,0:T(8,128)}, u32[]{:S(2)}) copy-start(f32[256,768]{1,0:T(8,128)} %copy-done.11) | copy-start | bytes 2359300
  248.3 8.1 %collective-permute-start.4 = (bf16[4,4,176,192]{3,2,1,0:T(8,128)(2,1)}, bf16[4,4,176,192]{3,2,1,0:T(8,128)(2,1)}, u32[]{:S(2)}, u32[]{:S(2)}) collective-permute-start(bf16[4,4,176,192]{3,2,1,0:T(8,128)(2,1)} %fusion.6), channel_id=1, source_target_pairs={{0,1},{1,0},{2,3},{3,2},{4,5},{5,4},{6,7},{7,6},{8,9},{9,8},{10,11... | collective-permute-start | bytes 3244040 | tf_op jit(solution)/shard_map/ppermute | solution.py:375
  249.0 7.4 %copy-start.15 = (f32[2,4,320,192]{3,2,1,0:T(8,128)S(1)}, f32[2,4,320,192]{3,2,1,0:T(8,128)}, u32[]{:S(2)}) copy-start(f32[2,4,320,192]{3,2,1,0:T(8,128)} %copy-done.14) | copy-start | bytes 5898244
  249.1 13.3 %collective-permute-start.10 = (bf16[256,768]{1,0:T(8,128)(2,1)S(1)}, bf16[256,768]{1,0:T(8,128)(2,1)S(1)}, u32[]{:S(2)}, u32[]{:S(2)}) collective-permute-start(bf16[256,768]{1,0:T(8,128)(2,1)S(1)} %get-tuple-element.96), channel_id=1, source_target_pairs={{0,6},{2,0},{4,2},{6,4},{1,7},{3,1},{5,3},{7,5},{8,14},{10,8},{12,... | collective-permute-start | bytes 1179656 | tf_op jit(solution)/shard_map/ppermute | solution.py:375
  252.9 19.0 %collective-permute-start.8 = (bf16[256,768]{1,0:T(8,128)(2,1)S(1)}, bf16[256,768]{1,0:T(8,128)(2,1)S(1)}, u32[]{:S(2)}, u32[]{:S(2)}) collective-permute-start(bf16[256,768]{1,0:T(8,128)(2,1)S(1)} %get-tuple-element.95), channel_id=1, source_target_pairs={{0,2},{2,4},{4,6},{6,0},{1,3},{3,5},{5,7},{7,1},{8,10},{10,12},{12... | collective-permute-start | bytes 1179656 | tf_op jit(solution)/shard_map/ppermute | solution.py:375
  253.0 34.3 %collective-permute-start.9 = (bf16[256,768]{1,0:T(8,128)(2,1)S(1)}, bf16[256,768]{1,0:T(8,128)(2,1)S(1)}, u32[]{:S(2)}, u32[]{:S(2)}) collective-permute-start(bf16[256,768]{1,0:T(8,128)(2,1)S(1)} %get-tuple-element.97), channel_id=1, source_target_pairs={{0,4},{2,6},{4,0},{6,2},{1,5},{3,7},{5,1},{7,3},{8,12},{10,14},{12... | collective-permute-start | bytes 1179656 | tf_op jit(solution)/shard_map/ppermute | solution.py:375
  258.8 28.6 %collective-permute-start.5 = (bf16[4,176,192]{2,1,0:T(8,128)(2,1)S(1)}, bf16[4,176,192]{2,1,0:T(8,128)(2,1)S(1)}, u32[]{:S(2)}, u32[]{:S(2)}) collective-permute-start(bf16[4,176,192]{2,1,0:T(8,128)(2,1)S(1)} %get-tuple-element.90), channel_id=1, source_target_pairs={{0,8},{8,16},{16,24},{24,0},{1,9},{9,17},{17,25},{25,1},{2,10},{10... | collective-permute-start | bytes 811016 | tf_op jit(solution)/shard_map/ppermute | solution.py:375
  260.7 26.7 %collective-permute-start.6 = (bf16[4,176,192]{2,1,0:T(8,128)(2,1)S(1)}, bf16[4,176,192]{2,1,0:T(8,128)(2,1)S(1)}, u32[]{:S(2)}, u32[]{:S(2)}) collective-permute-start(bf16[4,176,192]{2,1,0:T(8,128)(2,1)S(1)} %get-tuple-element.92), channel_id=1, source_target_pairs={{0,16},{8,24},{16,0},{24,8},{1,17},{9,25},{17,1},{25,9},{2,18},{10... | collective-permute-start | bytes 811016 | tf_op jit(solution)/shard_map/ppermute | solution.py:375
  262.4 25.0 %collective-permute-start.7 = (bf16[4,176,192]{2,1,0:T(8,128)(2,1)S(1)}, bf16[4,176,192]{2,1,0:T(8,128)(2,1)S(1)}, u32[]{:S(2)}, u32[]{:S(2)}) collective-permute-start(bf16[4,176,192]{2,1,0:T(8,128)(2,1)S(1)} %get-tuple-element.91), channel_id=1, source_target_pairs={{0,24},{8,0},{16,8},{24,16},{1,25},{9,1},{17,9},{25,17},{2,26},{10... | collective-permute-start | bytes 811016 | tf_op jit(solution)/shard_map/ppermute | solution.py:375
  288.3 9.3 %copy-start.24 = (bf16[1,256,768]{2,1,0:T(8,128)(2,1)S(1)}, bf16[1,256,768]{2,1,0:T(8,128)(2,1)}, u32[]{:S(2)}) copy-start(bf16[1,256,768]{2,1,0:T(8,128)(2,1)} %param.14) | copy-start | bytes 1179652
  288.3 2.9 copy-start.30
  291.3 14.3 %copy-start.21 = (f32[256,768]{1,0:T(8,128)S(1)}, f32[256,768]{1,0:T(8,128)}, u32[]{:S(2)}) copy-start(f32[256,768]{1,0:T(8,128)} %copy-done.20) | copy-start | bytes 2359300
  291.3 14.3 %copy-start.29 = (bf16[1,256,768]{2,1,0:T(8,128)(2,1)S(1)}, bf16[1,256,768]{2,1,0:T(8,128)(2,1)}, u32[]{:S(2)}) copy-start(bf16[1,256,768]{2,1,0:T(8,128)(2,1)} %param.15) | copy-start | bytes 1179652
  291.3 7.4 %collective-permute-start.11 = (bf16[176,192]{1,0:T(8,128)(2,1)S(1)}, bf16[176,192]{1,0:T(8,128)(2,1)S(1)}, u32[]{:S(2)}, u32[]{:S(2)}) collective-permute-start(bf16[176,192]{1,0:T(8,128)(2,1)S(1)} %get-tuple-element.111), channel_id=1, source_target_pairs={{0,2},{2,4},{4,6},{6,0},{1,3},{3,5},{5,7},{7,1},{8,10},{10,12},{12... | collective-permute-start | bytes 202760 | tf_op jit(solution)/shard_map/ppermute | solution.py:390
  295.2 6.6 %collective-permute-start.12 = (bf16[176,192]{1,0:T(8,128)(2,1)S(1)}, bf16[176,192]{1,0:T(8,128)(2,1)S(1)}, u32[]{:S(2)}, u32[]{:S(2)}) collective-permute-start(bf16[176,192]{1,0:T(8,128)(2,1)S(1)} %get-tuple-element.110), channel_id=1, source_target_pairs={{0,4},{2,6},{4,0},{6,2},{1,5},{3,7},{5,1},{7,3},{8,12},{10,14},{12... | collective-permute-start | bytes 202760 | tf_op jit(solution)/shard_map/ppermute | solution.py:390
  295.2 6.6 %collective-permute-start.13 = (bf16[176,192]{1,0:T(8,128)(2,1)S(1)}, bf16[176,192]{1,0:T(8,128)(2,1)S(1)}, u32[]{:S(2)}, u32[]{:S(2)}) collective-permute-start(bf16[176,192]{1,0:T(8,128)(2,1)S(1)} %get-tuple-element.109), channel_id=1, source_target_pairs={{0,6},{2,0},{4,2},{6,4},{1,7},{3,1},{5,3},{7,5},{8,14},{10,8},{12,... | collective-permute-start | bytes 202760 | tf_op jit(solution)/shard_map/ppermute | solution.py:390
  302.0 8.4 %collective-permute-start.14 = (bf16[416,192]{1,0:T(8,128)(2,1)S(1)}, bf16[416,192]{1,0:T(8,128)(2,1)}, u32[]{:S(2)}, u32[]{:S(2)}) collective-permute-start(bf16[416,192]{1,0:T(8,128)(2,1)S(1)} %fusion.43), channel_id=1, source_target_pairs={{0,8},{8,16},{16,24},{24,0},{1,9},{9,17},{17,25},{25,1},{2,10},{10... | collective-permute-start | bytes 479240 | tf_op jit(solution)/shard_map/ppermute | solution.py:390
  302.6 9.2 %collective-permute-start.15 = (bf16[416,192]{1,0:T(8,128)(2,1)S(1)}, bf16[416,192]{1,0:T(8,128)(2,1)}, u32[]{:S(2)}, u32[]{:S(2)}) collective-permute-start(bf16[416,192]{1,0:T(8,128)(2,1)S(1)} %fusion.43), channel_id=1, source_target_pairs={{0,16},{8,24},{16,0},{24,8},{1,17},{9,25},{17,1},{25,9},{2,18},{10... | collective-permute-start | bytes 479240 | tf_op jit(solution)/shard_map/ppermute | solution.py:390
  304.3 9.5 %collective-permute-start.16 = (bf16[416,192]{1,0:T(8,128)(2,1)S(1)}, bf16[416,192]{1,0:T(8,128)(2,1)}, u32[]{:S(2)}, u32[]{:S(2)}) collective-permute-start(bf16[416,192]{1,0:T(8,128)(2,1)S(1)} %fusion.43), channel_id=1, source_target_pairs={{0,24},{8,0},{16,8},{24,16},{1,25},{9,1},{17,9},{25,17},{2,26},{10... | collective-permute-start | bytes 479240 | tf_op jit(solution)/shard_map/ppermute | solution.py:390
  315.1 4.3 %copy-start.1 = (bf16[96,768]{1,0:T(8,128)(2,1)S(1)}, bf16[96,768]{1,0:T(8,128)(2,1)}, u32[]{:S(2)}) copy-start(bf16[96,768]{1,0:T(8,128)(2,1)} %param.20) | copy-start | bytes 442372
Sparse Core Ops, SparseCore 0:
  9.9 70.3 all-gather.2
  82.2 57.0 all-gather.4
  168.3 56.0 reduce-scatter.2
  227.3 64.3 reduce-scatter.4
